TPU v7x, 32 devices: a whole 2x2x4 slice. The times are simulated.
32 devices in a mesh: slab: 4 (over z), tile: 8 (over y, x, core).
Axes of the slice: x: 2, y: 2, z: 4, core: 2. Of those that a mesh axis runs over, the one named last changes fastest.
Arguments:
- features: bfloat16 [256, 64, 512], P(('slab', 'tile')), may hold values from -6 to 6
- cotangent: bfloat16 [256, 64, 512], P(('slab', 'tile')), may hold values from -6 to 6
- weight: bfloat16 [64, 1728], replicated, may hold values from -0.15625 to 0.15625
- block_table: int32 [4, 16, 8], replicated, may hold values from -1 to 7, as said below
Outputs:
- conv_out: bfloat16 [256, 64, 512], P(('slab', 'tile'))
- grad_features: bfloat16 [256, 64, 512], P(('slab', 'tile'))
- grad_weight: float32 [64, 1728], replicated
Inputs may be any that keep to these rules, and one draw needn't show every extreme that they name: `block_table`: -1 marks an inactive block. An active block (bz, by, bx) holds (by modulo 2) * 4 plus the number of active blocks before it along x in its row (bz, by). Every row has at least one and at most 4 active blocks; all rows of one block layer bz share an active block in one column. Some row with by modulo 2 = 1 has exactly 4.
All inputs are finite; a program needn't handle non-finite values.
Results may differ from a plain program's by a relative error of at most 0.001.
Values may be sent and summed in bfloat16 or wider, within the bound.
A program may use at most 64 MiB of HBM per device.

v0:
```python
import functools

import jax
import jax.numpy as jnp
from jax import lax
from jax.experimental import pallas as pl
from jax.experimental.pallas import tpu as pltpu
from jax.sharding import PartitionSpec as P

LZ = 1
YR = 2
LX = 8
CAPL = 4
CH = 64
SLOTS = LZ * YR * CAPL
PAIRS = 14
MESH = pl.DeviceIdType.MESH
F32 = jnp.float32
BF16 = jnp.bfloat16


def kernel(n_slab, n_tile, rows,
           tab, pos, valid, scale, x_ref, g_ref, w_ref,
           conv_ref, grad_ref, gw_ref,
           t_buf, d_buf, c_buf, acc, zs, zr, ys, yr, es, er,
           pay, rb1, s1, rb2, f1, fb,
           hs_sem, hr_sem, a_s, a_r, b_s, b_r, c_s, c_r, e_s, e_r):
    slab = lax.axis_index("slab")
    tile = lax.axis_index("tile")
    ch1 = rows // n_tile
    ch2 = ch1 // n_slab

    def has(dz, dt):
        ok = None
        for v, d, n in ((slab, dz, n_slab), (tile, dt, n_tile)):
            if d:
                c = (v > 0) if d < 0 else (v < n - 1)
                ok = c if ok is None else jnp.logical_and(ok, c)
        return ok

    barrier = pltpu.get_barrier_semaphore()
    for d in range(1, n_tile):
        pl.semaphore_signal(barrier, inc=1, device_id=(slab, lax.rem(tile + d, n_tile)), device_id_type=MESH)
    for d in range(1, n_slab):
        pl.semaphore_signal(barrier, inc=1, device_id=(lax.rem(slab + d, n_slab), tile), device_id_type=MESH)
    diagonals = [(dz, dt) for dz in (-1, 1) for dt in (-1, 1)]
    for dz, dt in diagonals:
        @pl.when(has(dz, dt))
        def _():
            pl.semaphore_signal(barrier, inc=1, device_id=(slab + dz, tile + dt), device_id_type=MESH)

    def to_rows(s, y_side):
        both = jnp.concatenate([x_ref[s].astype(F32), g_ref[s].astype(F32)], axis=0)
        r = both.T
        r4 = r.reshape(8, 8, 8, 2 * CH)
        t_buf[s] = r4
        zs[0, s] = r[0:64].astype(BF16)
        zs[1, s] = r[448:512].astype(BF16)
        yrow = 0 if y_side == 0 else 7
        q = s - CAPL * y_side
        ys[y_side, q] = r4[:, yrow].reshape(64, 2 * CH).astype(BF16)
        es[0, y_side, q] = r4[0, yrow]
        es[1, y_side, q] = r4[7, yrow]

    def lower(s, _):
        to_rows(s, 0)
        return 0

    def upper(s, _):
        to_rows(s, 1)
        return 0

    lax.fori_loop(0, CAPL, lower, 0)
    lax.fori_loop(CAPL, SLOTS, upper, 0)

    z_near = (slab > 0).astype(jnp.int32) + (slab < n_slab - 1).astype(jnp.int32)
    t_near = (tile > 0).astype(jnp.int32) + (tile < n_tile - 1).astype(jnp.int32)
    pl.semaphore_wait(barrier, n_tile - 1 + n_slab - 1 + z_near * t_near)

    dirs = [(dz, dt) for dz in (-1, 0, 1) for dt in (-1, 0, 1) if dz or dt]
    copies = {}
    for m, (dz, dt) in enumerate(dirs):
        zi, yi = (dz + 1) // 2, (dt + 1) // 2
        if dt == 0:
            src, dst = zs.at[zi], zr.at[1 - zi, pl.ds(0, SLOTS)]
        elif dz == 0:
            src, dst = ys.at[yi], yr.at[1 - yi, pl.ds(0, CAPL)]
        else:
            src, dst = es.at[zi, yi], er.at[1 - zi, 1 - yi, pl.ds(0, CAPL)]
        copies[(dz, dt)] = pltpu.make_async_remote_copy(
            src_ref=src, dst_ref=dst, send_sem=hs_sem.at[m], recv_sem=hr_sem.at[7 - m],
            device_id=(slab + dz, tile + dt), device_id_type=MESH)
    for m in dirs:
        @pl.when(has(*m))
        def _():
            copies[m].start()

    t_buf[SLOTS] = jnp.zeros((8, 8, 8, 2 * CH), F32)
    for side in range(2):
        zr[side, SLOTS] = jnp.zeros((64, 2 * CH), BF16)
        yr[side, CAPL] = jnp.zeros((64, 2 * CH), BF16)
        for other in range(2):
            er[side, other, CAPL] = jnp.zeros((8, 2 * CH), F32)

    def clear(z, _):
        d_buf[0, z] = jnp.zeros((18, 8, 2 * CH), F32)
        d_buf[LX + 1, z] = jnp.zeros((18, 8, 2 * CH), F32)
        return 0

    lax.fori_loop(0, 10, clear, 0)

    def inner(b, _):
        for ly in range(YR):
            i = tab[1, 1 + ly, b]
            d_buf[b + 1, 1:9, 1 + 8 * ly:9 + 8 * ly] = t_buf[i]
        return 0

    lax.fori_loop(0, LX, inner, 0)

    for m in dirs:
        @pl.when(has(*m))
        def _():
            copies[(-m[0], -m[1])].wait_recv()

    def outer(b, _):
        for zi in range(2):
            for ly in range(YR):
                i = tab[2 * zi, 1 + ly, b]
                d_buf[b + 1, 9 * zi, 1 + 8 * ly:9 + 8 * ly] = zr[zi, i].astype(F32).reshape(8, 8, 2 * CH)
            for yi in range(2):
                i = tab[2 * zi, 3 * yi, b]
                d_buf[b + 1, 9 * zi, 17 * yi] = er[zi, yi, i]
        for yi in range(2):
            i = tab[1, 3 * yi, b]
            d_buf[b + 1, 1:9, 17 * yi] = yr[yi, i].astype(F32).reshape(8, 8, 2 * CH)
        return 0

    lax.fori_loop(0, LX, outer, 0)

    acc[...] = jnp.zeros_like(acc)

    def first(s, _):
        b = pos[s]
        y0 = s // CAPL * 8

        def plane(z, _):
            mid = d_buf[b + 1, z, pl.ds(y0, 10)]
            left = d_buf[b, z, pl.ds(y0, 10)]
            right = d_buf[b + 2, z, pl.ds(y0, 10)]
            row = lax.broadcasted_iota(jnp.int32, (10, 8, 2 * CH), 1)
            shifted = (
                pltpu.roll(jnp.where(row == 7, left, mid), 1, 1),
                mid,
                pltpu.roll(jnp.where(row == 0, right, mid), 7, 1),
            )
            for dy in range(3):
                for dx in range(3):
                    j = dy * 3 + dx
                    c_buf[s, pl.ds(pl.multiple_of(z * 64, 64), 64), j * 128:(j + 1) * 128] = (
                        shifted[dx][dy:dy + 8].reshape(64, 2 * CH).astype(BF16))
            return 0

        lax.fori_loop(0, 10, plane, 0)
        g = g_ref[s].astype(F32) * valid[s]
        wide = jnp.concatenate([g, jnp.zeros((CH, 128), F32)], axis=1)
        lhs = jnp.concatenate([wide, pltpu.roll(wide, 64, 1), pltpu.roll(wide, 128, 1)], axis=0).astype(BF16)
        acc[...] += jnp.dot(lhs, c_buf[s], preferred_element_type=F32)
        return 0

    lax.fori_loop(0, SLOTS, first, 0)

    lane = lax.broadcasted_iota(jnp.int32, (CH, 128), 1)

    def term(k):
        dz, j = divmod(k, 9)
        return acc[dz * 64:(dz + 1) * 64, j * 128:(j + 1) * 128]

    for p in range(PAIRS):
        other = pltpu.roll(term(2 * p + 1), 64, 1) if 2 * p + 1 < 27 else jnp.zeros((CH, 128), F32)
        pay[p * 64:(p + 1) * 64] = jnp.where(lane < 64, term(2 * p), other)
    pay[PAIRS * 64:] = jnp.zeros((rows - PAIRS * 64, 128), F32)

    def second(s, _):
        r = jnp.dot(c_buf[s], w_ref[...], preferred_element_type=F32)
        o = (r[0:512, 0:128] + r[64:576, 128:256] + r[128:640, 256:384]) * valid[s]
        ot = o.T
        conv_ref[s] = ot[0:CH].astype(BF16)
        grad_ref[s] = ot[CH:2 * CH].astype(BF16)
        return 0

    step1 = []
    for d in range(1, n_tile):
        peer = lax.rem(tile + d, n_tile)
        step1.append(pltpu.make_async_remote_copy(
            src_ref=pay.at[pl.ds(pl.multiple_of(peer * ch1, 8), ch1)], dst_ref=rb1.at[d],
            send_sem=a_s.at[d], recv_sem=a_r.at[d], device_id=(slab, peer), device_id_type=MESH))
    for c in step1:
        c.start()
    lax.fori_loop(0, 3, second, 0)
    for c in step1:
        c.wait_recv()
    total = pay[pl.ds(pl.multiple_of(tile * ch1, 8), ch1)]
    for d in range(1, n_tile):
        total = total + rb1[d]
    s1[...] = total

    step2 = []
    for d in range(1, n_slab):
        peer = lax.rem(slab + d, n_slab)
        step2.append(pltpu.make_async_remote_copy(
            src_ref=s1.at[pl.ds(pl.multiple_of(peer * ch2, 8), ch2)], dst_ref=rb2.at[d],
            send_sem=b_s.at[d], recv_sem=b_r.at[d], device_id=(peer, tile), device_id_type=MESH))
    for c in step2:
        c.start()
    lax.fori_loop(3, 4, second, 0)
    for c in step2:
        c.wait_recv()
    mine = pl.ds(pl.multiple_of(slab * ch2, 8), ch2)
    total = s1[mine]
    for d in range(1, n_slab):
        total = total + rb2[d]
    f1[mine] = total * scale[0]

    step3 = []
    for d in range(1, n_slab):
        step3.append(pltpu.make_async_remote_copy(
            src_ref=f1.at[mine], dst_ref=f1.at[mine],
            send_sem=c_s.at[d], recv_sem=c_r.at[d],
            device_id=(lax.rem(slab + d, n_slab), tile), device_id_type=MESH))
    for c in step3:
        c.start()
    lax.fori_loop(4, 5, second, 0)
    for c in step3:
        c.wait_recv()

    place = pl.ds(pl.multiple_of(tile * ch1, 8), ch1)
    step4 = []
    for d in range(1, n_tile):
        step4.append(pltpu.make_async_remote_copy(
            src_ref=f1, dst_ref=fb.at[place],
            send_sem=e_s.at[d], recv_sem=e_r.at[d],
            device_id=(slab, lax.rem(tile + d, n_tile)), device_id_type=MESH))
    for c in step4:
        c.start()
    fb[place] = f1[...]
    lax.fori_loop(5, SLOTS, second, 0)
    for c in step4:
        c.wait_recv()
    for p in range(PAIRS - 1):
        gw_ref[:, p * 128:(p + 1) * 128] = fb[p * 64:(p + 1) * 64]
    gw_ref[:, (PAIRS - 1) * 128:] = fb[(PAIRS - 1) * 64:PAIRS * 64, 0:64]

    for c in step1 + step2 + step3 + step4:
        c.wait_send()
    for m in dirs:
        @pl.when(has(*m))
        def _():
            copies[m].wait_send()


def shards(n_slab, n_tile, features, cotangent, weight, block_table):
    slab = lax.axis_index("slab")
    tile = lax.axis_index("tile")
    padded = jnp.pad(block_table, ((1, 1), (1, 1), (0, 0)), constant_values=-1)
    near = lax.dynamic_slice(padded, (slab * LZ, tile * YR, 0), (3, YR + 2, LX))
    lead = jnp.array([CAPL, 0, 0, 0], jnp.int32)[None, :, None]
    none = jnp.array([CAPL, SLOTS, SLOTS, CAPL], jnp.int32)[None, :, None]
    tab = jnp.where(near >= 0, near - lead, none)
    own = near[1, 1:1 + YR]
    slot_ids = jnp.arange(SLOTS, dtype=jnp.int32)
    matches = own.reshape(1, YR * LX) == slot_ids[:, None]
    pos = jnp.sum(jnp.where(matches, jnp.arange(YR * LX, dtype=jnp.int32)[None, :] % LX, 0), axis=1)
    valid = jnp.any(matches, axis=1).astype(F32)
    voxels = jnp.sum((block_table >= 0).astype(F32)) * 512.0
    scale = (1.0 / jnp.sqrt(voxels)).reshape(1)

    fw = weight.reshape(CH, 3, 9, CH).transpose(2, 3, 1, 0)
    bw = weight.reshape(CH, 27, CH)[:, ::-1].reshape(CH, 3, 9, CH).transpose(2, 0, 1, 3)
    zero = jnp.zeros_like(fw)
    big = jnp.concatenate(
        [jnp.concatenate([fw, zero], axis=3), jnp.concatenate([zero, bw], axis=3)], axis=1
    ).reshape(9 * 2 * CH, 3 * 2 * CH)

    unit = 8 * n_slab * n_tile
    rows = -(-PAIRS * 64 // unit) * unit
    ch1 = rows // n_tile
    ch2 = ch1 // n_slab
    vmem = pl.BlockSpec(memory_space=pltpu.VMEM)
    smem = pl.BlockSpec(memory_space=pltpu.SMEM)
    dma = pltpu.SemaphoreType.DMA
    flops = 2 * SLOTS * 640 * 1152 * (384 + 192)
    return pl.pallas_call(
        functools.partial(kernel, n_slab, n_tile, rows),
        out_shape=(
            jax.ShapeDtypeStruct((SLOTS, CH, 512), BF16),
            jax.ShapeDtypeStruct((SLOTS, CH, 512), BF16),
            jax.ShapeDtypeStruct((CH, 27 * CH), F32),
        ),
        in_specs=[smem] * 4 + [vmem] * 3,
        out_specs=(vmem, vmem, vmem),
        scratch_shapes=[
            pltpu.VMEM((SLOTS + 1, 8, 8, 8, 128), F32),
            pltpu.VMEM((LX + 2, 10, 18, 8, 128), F32),
            pltpu.VMEM((SLOTS, 640, 1152), BF16),
            pltpu.VMEM((192, 1152), F32),
            pltpu.VMEM((2, SLOTS, 64, 128), BF16),
            pltpu.VMEM((2, SLOTS + 1, 64, 128), BF16),
            pltpu.VMEM((2, CAPL, 64, 128), BF16),
            pltpu.VMEM((2, CAPL + 1, 64, 128), BF16),
            pltpu.VMEM((2, 2, CAPL, 8, 128), F32),
            pltpu.VMEM((2, 2, CAPL + 1, 8, 128), F32),
            pltpu.VMEM((rows, 128), F32),
            pltpu.VMEM((n_tile, ch1, 128), F32),
            pltpu.VMEM((ch1, 128), F32),
            pltpu.VMEM((n_slab, ch2, 128), F32),
            pltpu.VMEM((ch1, 128), F32),
            pltpu.VMEM((rows, 128), F32),
            dma((8,)), dma((8,)),
            dma((n_tile,)), dma((n_tile,)),
            dma((n_slab,)), dma((n_slab,)),
            dma((n_slab,)), dma((n_slab,)),
            dma((n_tile,)), dma((n_tile,)),
        ],
        compiler_params=pltpu.CompilerParams(
            collective_id=0, has_side_effects=True, vmem_limit_bytes=48 * 1024 * 1024
        ),
        cost_estimate=pl.CostEstimate(flops=flops, bytes_accessed=3 << 20, transcendentals=0),
    )(tab, pos, valid, scale, features, cotangent, big)


def solution(mesh):
    placed = (P(("slab", "tile"), None, None), P(("slab", "tile"), None, None), P(), P())
    return jax.shard_map(
        functools.partial(shards, mesh.shape["slab"], mesh.shape["tile"]),
        mesh=mesh,
        in_specs=placed,
        out_specs=(P(("slab", "tile"), None, None), P(("slab", "tile"), None, None), P()),
        check_vma=False,
    )
```

profile of v0, /device:TPU:0, one launch (start us, length us, event | category | flops | bytes accessed | tf_op | source)
XLA Modules:
  0.0 52.9 jit_solution(16355930361848787596)
XLA Ops:
  0.6 1.3 %convert_reduce_fusion = f32[]{:T(128)} fusion(s32[4,16,8]{1,2,0:T(8,128)} %param.9), kind=kLoop, calls=%fused_computation.8 | loop fusion | flops 1535 | bytes 2052 | tf_op jit(solution)/shard_map/reduce_sum | solution.py:274
  2.7 0.8 %copy.15 = s32[4,16,8]{2,1,0:T(8,128)S(1)} copy(s32[4,16,8]{1,2,0:T(8,128)} %param.9) | data formatting | bytes 4096 | tf_op args[3]
  3.5 0.8 %add_select_fusion.tab = s32[3,4,8]{2,1,0:T(4,128)S(1)} fusion(s32[]{:T(128)S(6)} %select_n.26, s32[]{:T(128)S(6)} %select_n.27, s32[4,16,8]{2,1,0:T(8,128)S(1)} %copy.15, s32[4]{0:T(128)} %constant.58, s32[4]{0:T(128)} %constant.49.clone), kind=kLoop, calls=%fused_computation.9 | loop fusion | flops 288 | bytes 2472 | tf_op jit(solution)/shard_map/jit(_where)/select_n | solution.py:268
  4.2 0.1 eq.17
  4.3 0.1 select_reduce_fusion.pos
  4.4 0.1 fusion.3
  4.6 1.2 %copy.16 = bf16[64,1728]{0,1:T(8,128)(2,1)S(1)} copy(bf16[64,1728]{1,0:T(8,128)(2,1)} %param.8) | data formatting | bytes 442368 | tf_op args[2]
  5.8 1.4 %reshape.41 = bf16[64,27,64]{2,1,0:T(8,128)(2,1)S(1)} reshape(bf16[64,1728]{1,0:T(8,128)(2,1)} %param.8) | data formatting | bytes 442368 | tf_op jit(solution)/shard_map/reshape | solution.py:278
  7.2 0.5 %rev.3 = bf16[64,27,64]{2,1,0:T(8,128)(2,1)S(1)} reverse(bf16[64,27,64]{2,1,0:T(8,128)(2,1)S(1)} %reshape.41), dimensions={1} | reverse | bytes 442368 | tf_op jit(solution)/shard_map/rev | solution.py:278
  7.7 0.2 copy.17
  7.9 0.3 fusion.2
  8.2 0.8 %copy.18 = bf16[9,128,3,128]{3,2,1,0:T(4,128)(2,1)S(1)} copy(bf16[9,128,3,128]{3,1,0,2:T(8,128)(2,1)S(1)} %fusion.2) | data formatting | bytes 1769472 | tf_op jit(solution)/shard_map/concatenate | solution.py:280
  8.9 0.0 copy-start
  9.0 0.0 copy-start.1
  9.0 0.1 copy.21
  9.1 0.9 %copy-done = bf16[8,64,512]{2,1,0:T(8,128)(2,1)S(1)} copy-done((bf16[8,64,512]{2,1,0:T(8,128)(2,1)S(1)}, bf16[8,64,512]{2,1,0:T(8,128)(2,1)}, u32[]{:S(2)}) %copy-start) | copy-done | bytes 524312
  10.0 0.2 copy-done.1
  10.1 40.4 %shard_map.85 = (bf16[8,64,512]{2,1,0:T(8,128)(2,1)S(1)}, bf16[8,64,512]{2,1,0:T(8,128)(2,1)S(1)}, f32[64,1728]{1,0:T(8,128)S(1)}) custom-call(s32[3,4,8]{2,1,0:T(4,128)S(1)} %add_select_fusion.tab, s32[8]{0:T(128)S(1)} %select_reduce_fusion.pos, f32[8]{0:T(128)S(1)} %convert_element_type.6.valid, f32[1]{0:T(128)} %bitcast.scale, ...), custom_call_target="tpu_custom_call" | custom-call | flops 6794772480 | bytes 3145728 | tf_op jit(solution)/shard_map/pallas_call | solution.py:292
  50.5 0.8 %copy.25 = bf16[8,64,512]{2,1,0:T(8,128)(2,1)} copy(bf16[8,64,512]{2,1,0:T(8,128)(2,1)S(1)} %get-tuple-element.6) | data formatting | bytes 1048576
  51.3 0.8 %copy.26 = bf16[8,64,512]{2,1,0:T(8,128)(2,1)} copy(bf16[8,64,512]{2,1,0:T(8,128)(2,1)S(1)} %get-tuple-element.7) | data formatting | bytes 1048576
  52.1 0.8 %copy.27 = f32[64,1728]{1,0:T(8,128)} copy(f32[64,1728]{1,0:T(8,128)S(1)} %get-tuple-element.8) | data formatting | bytes 884736
  (3 shorter events, 0.0 us)
Async XLA Ops:
  8.9 1.0 %copy-start = (bf16[8,64,512]{2,1,0:T(8,128)(2,1)S(1)}, bf16[8,64,512]{2,1,0:T(8,128)(2,1)}, u32[]{:S(2)}) copy-start(bf16[8,64,512]{2,1,0:T(8,128)(2,1)} %x_ref.1) | copy-start | bytes 1572868
  9.0 1.2 %copy-start.1 = (bf16[8,64,512]{2,1,0:T(8,128)(2,1)S(1)}, bf16[8,64,512]{2,1,0:T(8,128)(2,1)}, u32[]{:S(2)}) copy-start(bf16[8,64,512]{2,1,0:T(8,128)(2,1)} %g_ref.1) | copy-start | bytes 1572868
where the time goes:
time: 53.3 us; the launch traced here: 52.9 us
  Pallas kernels  40.4 us (76%)
  local copies, waits for them, and re-layouts  8.51 us (16%)
  other arithmetic  2.58 us (5%)
  between operations  1.42 us (3%)
    pallas_call x1, Pallas kernels, shards(): pl.pallas_call(functools.partial(kernel, n_slab, n_tile, rows), out_shape...  40.4 us
    unnamed x10, local copies, waits for them, and re-layouts  5.53 us
    reshape x1, local copies, waits for them, and re-layouts, shards(): weight.reshape(CH, 27, CH)[:, ::-1].reshape(CH, 3, 9, CH)  1.42 us
    reduce_sum x1, other arithmetic, shards(): voxels = jnp.sum((block_table >= 0).astype(F32)) * 512.0  1.33 us

commit v1 on v0

--- a/solution.py
+++ b/solution.py
@@ -20,9 +20,10 @@
 
 
 def kernel(n_slab, n_tile, rows,
-           tab, pos, valid, scale, x_ref, g_ref, w_ref,
+           table, x_any, g_any, w_any, table_any,
            conv_ref, grad_ref, gw_ref,
-           t_buf, d_buf, c_buf, acc, zs, zr, ys, yr, es, er,
+           x_ref, g_ref, w_ref, table_v, in_sem, pos, valid, w_big,
+           t_buf, d_buf, c_even, c_odd, acc, zs, zr, ys, yr, es, er,
            pay, rb1, s1, rb2, f1, fb,
            hs_sem, hr_sem, a_s, a_r, b_s, b_r, c_s, c_r, e_s, e_r):
     slab = lax.axis_index("slab")
@@ -37,6 +38,22 @@
                 c = (v > 0) if d < 0 else (v < n - 1)
                 ok = c if ok is None else jnp.logical_and(ok, c)
         return ok
+
+    loads = [
+        pltpu.make_async_copy(src, dst, in_sem.at[i])
+        for i, (src, dst) in enumerate(
+            ((x_any, x_ref), (g_any, g_ref), (w_any, w_ref), (table_any, table_v)))
+    ]
+    for c in loads:
+        c.start()
+
+    def near(zi, yi, b):
+        z = slab + zi - 1
+        y = tile * YR + yi - 1
+        inside = (z >= 0) & (z < n_slab) & (y >= 0) & (y < n_tile * YR)
+        v = table[jnp.clip(z, 0, n_slab - 1), b, jnp.clip(y, 0, n_tile * YR - 1)]
+        none = CAPL if yi in (0, YR + 1) else SLOTS
+        return jnp.where(inside & (v >= 0), jnp.maximum(v - (CAPL if yi == 0 else 0), 0), none)
 
     barrier = pltpu.get_barrier_semaphore()
     for d in range(1, n_tile):
@@ -62,16 +79,10 @@
         es[0, y_side, q] = r4[0, yrow]
         es[1, y_side, q] = r4[7, yrow]
 
-    def lower(s, _):
-        to_rows(s, 0)
-        return 0
-
-    def upper(s, _):
-        to_rows(s, 1)
-        return 0
-
-    lax.fori_loop(0, CAPL, lower, 0)
-    lax.fori_loop(CAPL, SLOTS, upper, 0)
+    for c in loads[:2]:
+        c.wait()
+    for s in range(SLOTS):
+        to_rows(s, s // CAPL)
 
     z_near = (slab > 0).astype(jnp.int32) + (slab < n_slab - 1).astype(jnp.int32)
     t_near = (tile > 0).astype(jnp.int32) + (tile < n_tile - 1).astype(jnp.int32)
@@ -95,6 +106,36 @@
         def _():
             copies[m].start()
 
+    for s in range(SLOTS):
+        at, found = jnp.int32(0), jnp.float32(0)
+        for b in range(LX):
+            hit = table[slab, b, tile * YR + s // CAPL] == s
+            at = jnp.where(hit, b, at)
+            found = jnp.where(hit, 1.0, found)
+        pos[s] = at
+        valid[s] = found
+
+    for c in loads[2:]:
+        c.wait()
+    wide_lane = lax.broadcasted_iota(jnp.int32, (CH, 128), 1)
+    for p in range(PAIRS):
+        if p < PAIRS - 1:
+            pair = w_ref[:, p * 128:(p + 1) * 128].astype(F32)
+        else:
+            pair = jnp.concatenate(
+                [w_ref[:, p * 128:27 * CH].astype(F32), jnp.zeros((CH, 64), F32)], axis=1)
+        flipped = jnp.concatenate([pair, jnp.zeros((CH, 128), F32)], axis=0).T
+        for k in (2 * p, 2 * p + 1):
+            if k >= 27:
+                continue
+            dz, j = divmod(k, 9)
+            w_big[j * 128:j * 128 + 64, dz * 128:(dz + 1) * 128] = (
+                flipped[k % 2 * 64:k % 2 * 64 + 64].astype(BF16))
+            dz, j = divmod(26 - k, 9)
+            half = pair if k % 2 else pltpu.roll(pair, 64, 1)
+            w_big[j * 128 + 64:(j + 1) * 128, dz * 128:(dz + 1) * 128] = (
+                jnp.where(wide_lane >= 64, half, 0.0).astype(BF16))
+
     t_buf[SLOTS] = jnp.zeros((8, 8, 8, 2 * CH), F32)
     for side in range(2):
         zr[side, SLOTS] = jnp.zeros((64, 2 * CH), BF16)
@@ -111,7 +152,7 @@
 
     def inner(b, _):
         for ly in range(YR):
-            i = tab[1, 1 + ly, b]
+            i = near(1, 1 + ly, b)
             d_buf[b + 1, 1:9, 1 + 8 * ly:9 + 8 * ly] = t_buf[i]
         return 0
 
@@ -125,13 +166,13 @@
     def outer(b, _):
         for zi in range(2):
             for ly in range(YR):
-                i = tab[2 * zi, 1 + ly, b]
+                i = near(2 * zi, 1 + ly, b)
                 d_buf[b + 1, 9 * zi, 1 + 8 * ly:9 + 8 * ly] = zr[zi, i].astype(F32).reshape(8, 8, 2 * CH)
             for yi in range(2):
-                i = tab[2 * zi, 3 * yi, b]
+                i = near(2 * zi, 3 * yi, b)
                 d_buf[b + 1, 9 * zi, 17 * yi] = er[zi, yi, i]
         for yi in range(2):
-            i = tab[1, 3 * yi, b]
+            i = near(1, 3 * yi, b)
             d_buf[b + 1, 1:9, 17 * yi] = yr[yi, i].astype(F32).reshape(8, 8, 2 * CH)
         return 0
 
@@ -139,15 +180,14 @@
 
     acc[...] = jnp.zeros_like(acc)
 
-    def first(s, _):
+    def build(s, c_ref, q):
         b = pos[s]
         y0 = s // CAPL * 8
-
-        def plane(z, _):
+        row = lax.broadcasted_iota(jnp.int32, (10, 8, 2 * CH), 1)
+        for z in range(10):
             mid = d_buf[b + 1, z, pl.ds(y0, 10)]
             left = d_buf[b, z, pl.ds(y0, 10)]
             right = d_buf[b + 2, z, pl.ds(y0, 10)]
-            row = lax.broadcasted_iota(jnp.int32, (10, 8, 2 * CH), 1)
             shifted = (
                 pltpu.roll(jnp.where(row == 7, left, mid), 1, 1),
                 mid,
@@ -156,18 +196,25 @@
             for dy in range(3):
                 for dx in range(3):
                     j = dy * 3 + dx
-                    c_buf[s, pl.ds(pl.multiple_of(z * 64, 64), 64), j * 128:(j + 1) * 128] = (
+                    c_ref[q, z * 64:(z + 1) * 64, j * 128:(j + 1) * 128] = (
                         shifted[dx][dy:dy + 8].reshape(64, 2 * CH).astype(BF16))
-            return 0
-
-        lax.fori_loop(0, 10, plane, 0)
+
+    def terms(s, c_ref, q):
         g = g_ref[s].astype(F32) * valid[s]
         wide = jnp.concatenate([g, jnp.zeros((CH, 128), F32)], axis=1)
         lhs = jnp.concatenate([wide, pltpu.roll(wide, 64, 1), pltpu.roll(wide, 128, 1)], axis=0).astype(BF16)
-        acc[...] += jnp.dot(lhs, c_buf[s], preferred_element_type=F32)
-        return 0
-
-    lax.fori_loop(0, SLOTS, first, 0)
+        acc[...] += jnp.dot(lhs, c_ref[q], preferred_element_type=F32)
+
+    build(0, c_even, 0)
+
+    def first(q, _):
+        terms(2 * q, c_even, q)
+        build(2 * q + 1, c_odd, q)
+        terms(2 * q + 1, c_odd, q)
+        build(jnp.minimum(2 * q + 2, SLOTS - 1), c_even, q + 1)
+        return 0
+
+    lax.fori_loop(0, SLOTS // 2, first, 0)
 
     lane = lax.broadcasted_iota(jnp.int32, (CH, 128), 1)
 
@@ -180,12 +227,16 @@
         pay[p * 64:(p + 1) * 64] = jnp.where(lane < 64, term(2 * p), other)
     pay[PAIRS * 64:] = jnp.zeros((rows - PAIRS * 64, 128), F32)
 
-    def second(s, _):
-        r = jnp.dot(c_buf[s], w_ref[...], preferred_element_type=F32)
+    def second_of(s, c_ref, q):
+        r = jnp.dot(c_ref[q], w_big[...], preferred_element_type=F32)
         o = (r[0:512, 0:128] + r[64:576, 128:256] + r[128:640, 256:384]) * valid[s]
         ot = o.T
         conv_ref[s] = ot[0:CH].astype(BF16)
         grad_ref[s] = ot[CH:2 * CH].astype(BF16)
+
+    def second(q, _):
+        second_of(2 * q, c_even, q)
+        second_of(2 * q + 1, c_odd, q)
         return 0
 
     step1 = []
@@ -196,7 +247,7 @@
             send_sem=a_s.at[d], recv_sem=a_r.at[d], device_id=(slab, peer), device_id_type=MESH))
     for c in step1:
         c.start()
-    lax.fori_loop(0, 3, second, 0)
+    lax.fori_loop(0, 2, second, 0)
     for c in step1:
         c.wait_recv()
     total = pay[pl.ds(pl.multiple_of(tile * ch1, 8), ch1)]
@@ -212,14 +263,16 @@
             send_sem=b_s.at[d], recv_sem=b_r.at[d], device_id=(peer, tile), device_id_type=MESH))
     for c in step2:
         c.start()
-    lax.fori_loop(3, 4, second, 0)
+    second_of(4, c_even, 2)
     for c in step2:
         c.wait_recv()
     mine = pl.ds(pl.multiple_of(slab * ch2, 8), ch2)
     total = s1[mine]
     for d in range(1, n_slab):
         total = total + rb2[d]
-    f1[mine] = total * scale[0]
+    count = jnp.sum((table_v[...] >= 0).astype(F32), axis=0, keepdims=True)
+    count = jnp.sum(jnp.sum(count, axis=2, keepdims=True), axis=1, keepdims=True)[0]
+    f1[mine] = total / jnp.sqrt(count * 512.0)
 
     step3 = []
     for d in range(1, n_slab):
@@ -229,7 +282,7 @@
             device_id=(lax.rem(slab + d, n_slab), tile), device_id_type=MESH))
     for c in step3:
         c.start()
-    lax.fori_loop(4, 5, second, 0)
+    second_of(5, c_odd, 2)
     for c in step3:
         c.wait_recv()
 
@@ -243,7 +296,7 @@
     for c in step4:
         c.start()
     fb[place] = f1[...]
-    lax.fori_loop(5, SLOTS, second, 0)
+    lax.fori_loop(3, 4, second, 0)
     for c in step4:
         c.wait_recv()
     for p in range(PAIRS - 1):
@@ -259,28 +312,7 @@
 
 
 def shards(n_slab, n_tile, features, cotangent, weight, block_table):
-    slab = lax.axis_index("slab")
-    tile = lax.axis_index("tile")
-    padded = jnp.pad(block_table, ((1, 1), (1, 1), (0, 0)), constant_values=-1)
-    near = lax.dynamic_slice(padded, (slab * LZ, tile * YR, 0), (3, YR + 2, LX))
-    lead = jnp.array([CAPL, 0, 0, 0], jnp.int32)[None, :, None]
-    none = jnp.array([CAPL, SLOTS, SLOTS, CAPL], jnp.int32)[None, :, None]
-    tab = jnp.where(near >= 0, near - lead, none)
-    own = near[1, 1:1 + YR]
-    slot_ids = jnp.arange(SLOTS, dtype=jnp.int32)
-    matches = own.reshape(1, YR * LX) == slot_ids[:, None]
-    pos = jnp.sum(jnp.where(matches, jnp.arange(YR * LX, dtype=jnp.int32)[None, :] % LX, 0), axis=1)
-    valid = jnp.any(matches, axis=1).astype(F32)
-    voxels = jnp.sum((block_table >= 0).astype(F32)) * 512.0
-    scale = (1.0 / jnp.sqrt(voxels)).reshape(1)
-
-    fw = weight.reshape(CH, 3, 9, CH).transpose(2, 3, 1, 0)
-    bw = weight.reshape(CH, 27, CH)[:, ::-1].reshape(CH, 3, 9, CH).transpose(2, 0, 1, 3)
-    zero = jnp.zeros_like(fw)
-    big = jnp.concatenate(
-        [jnp.concatenate([fw, zero], axis=3), jnp.concatenate([zero, bw], axis=3)], axis=1
-    ).reshape(9 * 2 * CH, 3 * 2 * CH)
-
+    table = jnp.transpose(block_table, (0, 2, 1))
     unit = 8 * n_slab * n_tile
     rows = -(-PAIRS * 64 // unit) * unit
     ch1 = rows // n_tile
@@ -296,12 +328,21 @@
             jax.ShapeDtypeStruct((SLOTS, CH, 512), BF16),
             jax.ShapeDtypeStruct((CH, 27 * CH), F32),
         ),
-        in_specs=[smem] * 4 + [vmem] * 3,
+        in_specs=[smem] + [pl.BlockSpec(memory_space=pltpu.HBM)] * 4,
         out_specs=(vmem, vmem, vmem),
         scratch_shapes=[
+            pltpu.VMEM((SLOTS, CH, 512), BF16),
+            pltpu.VMEM((SLOTS, CH, 512), BF16),
+            pltpu.VMEM((CH, 27 * CH), BF16),
+            pltpu.VMEM(table.shape, jnp.int32),
+            dma((4,)),
+            pltpu.SMEM((SLOTS,), jnp.int32),
+            pltpu.SMEM((SLOTS,), F32),
+            pltpu.VMEM((1152, 384), BF16),
             pltpu.VMEM((SLOTS + 1, 8, 8, 8, 128), F32),
             pltpu.VMEM((LX + 2, 10, 18, 8, 128), F32),
-            pltpu.VMEM((SLOTS, 640, 1152), BF16),
+            pltpu.VMEM((SLOTS // 2 + 1, 640, 1152), BF16),
+            pltpu.VMEM((SLOTS // 2, 640, 1152), BF16),
             pltpu.VMEM((192, 1152), F32),
             pltpu.VMEM((2, SLOTS, 64, 128), BF16),
             pltpu.VMEM((2, SLOTS + 1, 64, 128), BF16),
@@ -325,7 +366,7 @@
             collective_id=0, has_side_effects=True, vmem_limit_bytes=48 * 1024 * 1024
         ),
         cost_estimate=pl.CostEstimate(flops=flops, bytes_accessed=3 << 20, transcendentals=0),
-    )(tab, pos, valid, scale, features, cotangent, big)
+    )(table, features, cotangent, weight, table)
 
 
 def solution(mesh):

time: 53.3 us -> 46.8 us (0.88)
  other arithmetic: 2.58 us -> 0 us
  local copies, waits for them, and re-layouts: 8.51 us -> 6.09 us
  between operations: 1.42 us -> 0.65 us
  Pallas kernels: 40.4 us -> 39.7 us
    reduce_sum x2 -> x0, other arithmetic: 1.45 us -> none  [the longest x1 1.33 us: shards(): voxels = jnp.sum((block_table >= 0).astype(F32)) * 512.0]
    reshape x1 -> x0, local copies, waits for them, and re-layouts: 1.42 us -> none  [shards(): weight.reshape(CH, 27, CH)[:, ::-1].reshape(CH, 3, 9, CH)]
    concatenate x1 -> x0, local copies, waits for them, and re-layouts: 0.76 us -> none  [shards(): jnp.concatenate([jnp.concatenate([fw, zero], axis=3), jnp.concatenate([ze...]
    select_n x2 -> x0, other arithmetic: 0.76 us -> none  [the longest x1 0.75 us: shards(): tab = jnp.where(near >= 0, near - lead, none)]
    rev x2 -> x0, local copies, waits for them, and re-layouts: 0.71 us -> none  [shards(): weight.reshape(CH, 27, CH)[:, ::-1].reshape(CH, 3, 9, CH)]
    pallas_call x1, Pallas kernels: 40.4 us -> 39.7 us  [shards(): pl.pallas_call(functools.partial(kernel, n_slab, n_tile, rows), out_shape...]
    unnamed x10 -> x11, local copies, waits for them, and re-layouts: 5.53 us -> 6.09 us
where the time goes in v1:
time: 46.8 us; the launch traced here: 46.4 us
  Pallas kernels  39.7 us (85%)
  local copies, waits for them, and re-layouts  6.09 us (13%)
  between operations  0.65 us (1%)
    pallas_call x1, Pallas kernels, shards(): pl.pallas_call(functools.partial(kernel, n_slab, n_tile, rows), out_shape...  39.7 us
    unnamed x11, local copies, waits for them, and re-layouts  6.09 us

profile of v1, /device:TPU:0, one launch (start us, length us, event | category | flops | bytes accessed | tf_op | source)
XLA Modules:
  0.0 46.4 jit_solution(16109864847085352202)
XLA Ops:
  0.6 0.0 copy-start
  0.6 1.0 %copy-done = bf16[8,64,512]{2,1,0:T(8,128)(2,1)S(1)} copy-done((bf16[8,64,512]{2,1,0:T(8,128)(2,1)S(1)}, bf16[8,64,512]{2,1,0:T(8,128)(2,1)}, u32[]{:S(2)}) %copy-start) | copy-done | bytes 524312
  1.7 0.0 copy-start.1
  1.7 1.0 %copy-done.1 = bf16[8,64,512]{2,1,0:T(8,128)(2,1)S(1)} copy-done((bf16[8,64,512]{2,1,0:T(8,128)(2,1)S(1)}, bf16[8,64,512]{2,1,0:T(8,128)(2,1)}, u32[]{:S(2)}) %copy-start.1) | copy-done | bytes 524312
  2.7 0.0 copy-start.2
  2.7 0.9 %copy-done.2 = bf16[64,1728]{1,0:T(8,128)(2,1)S(1)} copy-done((bf16[64,1728]{1,0:T(8,128)(2,1)S(1)}, bf16[64,1728]{1,0:T(8,128)(2,1)}, u32[]{:S(2)}) %copy-start.2) | copy-done | bytes 221208
  3.7 0.0 copy-start.3
  3.7 0.7 %copy-done.3 = s32[4,16,8]{1,2,0:T(8,128)S(1)} copy-done((s32[4,16,8]{1,2,0:T(8,128)S(1)}, s32[4,16,8]{1,2,0:T(8,128)}, u32[]{:S(2)}) %copy-start.3) | copy-done | bytes 2072
  4.4 39.7 %shard_map.67 = (bf16[8,64,512]{2,1,0:T(8,128)(2,1)S(1)}, bf16[8,64,512]{2,1,0:T(8,128)(2,1)S(1)}, f32[64,1728]{1,0:T(8,128)S(1)}) custom-call(s32[4,8,16]{2,1,0:T(8,128)S(1)} %bitcast.1, bf16[8,64,512]{2,1,0:T(8,128)(2,1)S(1)} %copy-done, bf16[8,64,512]{2,1,0:T(8,128)(2,1)S(1)} %copy-done.1, bf16[64,1728]{1,0:T(8,128)(2,1)S(1)} %copy-done.2, ...), custom_call_target="tpu_custom_call" | custom-call | flops 6794772480 | bytes 3145728 | tf_op jit(solution)/shard_map/pallas_call | solution.py:324
  44.1 0.8 %copy.10 = bf16[8,64,512]{2,1,0:T(8,128)(2,1)} copy(bf16[8,64,512]{2,1,0:T(8,128)(2,1)S(1)} %get-tuple-element.6) | data formatting | bytes 1048576
  44.9 0.8 %copy.11 = bf16[8,64,512]{2,1,0:T(8,128)(2,1)} copy(bf16[8,64,512]{2,1,0:T(8,128)(2,1)S(1)} %get-tuple-element.7) | data formatting | bytes 1048576
  45.7 0.8 %copy.12 = f32[64,1728]{1,0:T(8,128)} copy(f32[64,1728]{1,0:T(8,128)S(1)} %get-tuple-element.8) | data formatting | bytes 884736
Async XLA Ops:
  0.6 1.0 %copy-start = (bf16[8,64,512]{2,1,0:T(8,128)(2,1)S(1)}, bf16[8,64,512]{2,1,0:T(8,128)(2,1)}, u32[]{:S(2)}) copy-start(bf16[8,64,512]{2,1,0:T(8,128)(2,1)} %x_any.1) | copy-start | bytes 1572868
  1.7 1.0 %copy-start.1 = (bf16[8,64,512]{2,1,0:T(8,128)(2,1)S(1)}, bf16[8,64,512]{2,1,0:T(8,128)(2,1)}, u32[]{:S(2)}) copy-start(bf16[8,64,512]{2,1,0:T(8,128)(2,1)} %g_any.1) | copy-start | bytes 1572868
  2.7 0.9 %copy-start.2 = (bf16[64,1728]{1,0:T(8,128)(2,1)S(1)}, bf16[64,1728]{1,0:T(8,128)(2,1)}, u32[]{:S(2)}) copy-start(bf16[64,1728]{1,0:T(8,128)(2,1)} %w_any.1) | copy-start | bytes 663556
  3.7 0.7 %copy-start.3 = (s32[4,16,8]{1,2,0:T(8,128)S(1)}, s32[4,16,8]{1,2,0:T(8,128)}, u32[]{:S(2)}) copy-start(s32[4,16,8]{1,2,0:T(8,128)} %param.7) | copy-start | bytes 6148

commit v2 on v1

--- a/solution.py
+++ b/solution.py
@@ -14,23 +14,35 @@
 CH = 64
 SLOTS = LZ * YR * CAPL
 PAIRS = 14
+SHIFTS = ((0, 1, 2, 3, 4), (5, 6, 7, 8))
+
+
+def pairs_of(part):
+    ks = sorted(9 * dz + j for dz in range(3) for j in SHIFTS[part])
+    evens = [k for k in ks if k % 2 == 0]
+    odds = [k for k in ks if k % 2]
+    return [(k, odds[i] if i < len(odds) else None) for i, k in enumerate(evens)]
+
+
+def rows_of(part, n_tile):
+    unit = 8 * n_tile
+    return -(-len(pairs_of(part)) * 64 // unit) * unit
+
 MESH = pl.DeviceIdType.MESH
 F32 = jnp.float32
 BF16 = jnp.bfloat16
 
 
-def kernel(n_slab, n_tile, rows,
+def kernel(n_slab, n_tile,
            table, x_any, g_any, w_any, table_any,
            conv_ref, grad_ref, gw_ref,
            x_ref, g_ref, w_ref, table_v, in_sem, pos, valid, w_big,
            t_buf, d_buf, c_even, c_odd, acc, zs, zr, ys, yr, es, er,
-           pay, rb1, s1, rb2, f1, fb,
-           hs_sem, hr_sem, a_s, a_r, b_s, b_r, c_s, c_r, e_s, e_r):
+           pay_a, rb1_a, s1_a, rb2_a, f1_a, fb_a,
+           pay_b, rb1_b, s1_b, rb2_b, f1_b, fb_b,
+           hs_sem, hr_sem, tile_s, tile_r, slab_s, slab_r):
     slab = lax.axis_index("slab")
     tile = lax.axis_index("tile")
-    ch1 = rows // n_tile
-    ch2 = ch1 // n_slab
-
     def has(dz, dt):
         ok = None
         for v, d, n in ((slab, dz, n_slab), (tile, dt, n_tile)):
@@ -180,7 +192,7 @@
 
     acc[...] = jnp.zeros_like(acc)
 
-    def build(s, c_ref, q):
+    def build(s, c_ref, q, part):
         b = pos[s]
         y0 = s // CAPL * 8
         row = lax.broadcasted_iota(jnp.int32, (10, 8, 2 * CH), 1)
@@ -193,39 +205,29 @@
                 mid,
                 pltpu.roll(jnp.where(row == 0, right, mid), 7, 1),
             )
-            for dy in range(3):
-                for dx in range(3):
-                    j = dy * 3 + dx
-                    c_ref[q, z * 64:(z + 1) * 64, j * 128:(j + 1) * 128] = (
-                        shifted[dx][dy:dy + 8].reshape(64, 2 * CH).astype(BF16))
-
-    def terms(s, c_ref, q):
+            for j in SHIFTS[part]:
+                dy, dx = divmod(j, 3)
+                c_ref[q, z * 64:(z + 1) * 64, j * 128:(j + 1) * 128] = (
+                    shifted[dx][dy:dy + 8].reshape(64, 2 * CH).astype(BF16))
+
+    def terms(s, c_ref, q, part):
         g = g_ref[s].astype(F32) * valid[s]
         wide = jnp.concatenate([g, jnp.zeros((CH, 128), F32)], axis=1)
         lhs = jnp.concatenate([wide, pltpu.roll(wide, 64, 1), pltpu.roll(wide, 128, 1)], axis=0).astype(BF16)
-        acc[...] += jnp.dot(lhs, c_ref[q], preferred_element_type=F32)
-
-    build(0, c_even, 0)
-
-    def first(q, _):
-        terms(2 * q, c_even, q)
-        build(2 * q + 1, c_odd, q)
-        terms(2 * q + 1, c_odd, q)
-        build(jnp.minimum(2 * q + 2, SLOTS - 1), c_even, q + 1)
-        return 0
-
-    lax.fori_loop(0, SLOTS // 2, first, 0)
-
-    lane = lax.broadcasted_iota(jnp.int32, (CH, 128), 1)
-
-    def term(k):
-        dz, j = divmod(k, 9)
-        return acc[dz * 64:(dz + 1) * 64, j * 128:(j + 1) * 128]
-
-    for p in range(PAIRS):
-        other = pltpu.roll(term(2 * p + 1), 64, 1) if 2 * p + 1 < 27 else jnp.zeros((CH, 128), F32)
-        pay[p * 64:(p + 1) * 64] = jnp.where(lane < 64, term(2 * p), other)
-    pay[PAIRS * 64:] = jnp.zeros((rows - PAIRS * 64, 128), F32)
+        lo, hi = SHIFTS[part][0] * 128, SHIFTS[part][-1] * 128 + 128
+        acc[:, lo:hi] += jnp.dot(lhs, c_ref[q, :, lo:hi], preferred_element_type=F32)
+
+    def all_terms(part):
+        build(0, c_even, 0, part)
+
+        def step(q, _):
+            terms(2 * q, c_even, q, part)
+            build(2 * q + 1, c_odd, q, part)
+            terms(2 * q + 1, c_odd, q, part)
+            build(jnp.minimum(2 * q + 2, SLOTS - 1), c_even, q + 1, part)
+            return 0
+
+        lax.fori_loop(0, SLOTS // 2, step, 0)
 
     def second_of(s, c_ref, q):
         r = jnp.dot(c_ref[q], w_big[...], preferred_element_type=F32)
@@ -234,76 +236,109 @@
         conv_ref[s] = ot[0:CH].astype(BF16)
         grad_ref[s] = ot[CH:2 * CH].astype(BF16)
 
-    def second(q, _):
-        second_of(2 * q, c_even, q)
-        second_of(2 * q + 1, c_odd, q)
-        return 0
-
-    step1 = []
-    for d in range(1, n_tile):
-        peer = lax.rem(tile + d, n_tile)
-        step1.append(pltpu.make_async_remote_copy(
-            src_ref=pay.at[pl.ds(pl.multiple_of(peer * ch1, 8), ch1)], dst_ref=rb1.at[d],
-            send_sem=a_s.at[d], recv_sem=a_r.at[d], device_id=(slab, peer), device_id_type=MESH))
-    for c in step1:
-        c.start()
-    lax.fori_loop(0, 2, second, 0)
-    for c in step1:
-        c.wait_recv()
-    total = pay[pl.ds(pl.multiple_of(tile * ch1, 8), ch1)]
-    for d in range(1, n_tile):
-        total = total + rb1[d]
-    s1[...] = total
-
-    step2 = []
-    for d in range(1, n_slab):
-        peer = lax.rem(slab + d, n_slab)
-        step2.append(pltpu.make_async_remote_copy(
-            src_ref=s1.at[pl.ds(pl.multiple_of(peer * ch2, 8), ch2)], dst_ref=rb2.at[d],
-            send_sem=b_s.at[d], recv_sem=b_r.at[d], device_id=(peer, tile), device_id_type=MESH))
-    for c in step2:
-        c.start()
+    lane = lax.broadcasted_iota(jnp.int32, (CH, 128), 1)
+    bufs = ((pay_a, rb1_a, s1_a, rb2_a, f1_a, fb_a), (pay_b, rb1_b, s1_b, rb2_b, f1_b, fb_b))
+
+    def term(k):
+        dz, j = divmod(k, 9)
+        return acc[dz * 64:(dz + 1) * 64, j * 128:(j + 1) * 128]
+
+    def chunk(part):
+        return rows_of(part, n_tile) // n_tile
+
+    def own(part):
+        return pl.ds(pl.multiple_of(tile * chunk(part), 8), chunk(part))
+
+    def sum_tile_start(part):
+        pay, rb1 = bufs[part][:2]
+        used = len(pairs_of(part)) * 64
+        for p, (ke, ko) in enumerate(pairs_of(part)):
+            odd = jnp.zeros((CH, 128), F32) if ko is None else pltpu.roll(term(ko), 64, 1)
+            pay[p * 64:(p + 1) * 64] = jnp.where(lane < 64, term(ke), odd)
+        if rows_of(part, n_tile) > used:
+            pay[used:] = jnp.zeros((rows_of(part, n_tile) - used, 128), F32)
+        started = []
+        for d in range(1, n_tile):
+            peer = lax.rem(tile + d, n_tile)
+            started.append(pltpu.make_async_remote_copy(
+                src_ref=pay.at[pl.ds(pl.multiple_of(peer * chunk(part), 8), chunk(part))],
+                dst_ref=rb1.at[d], send_sem=tile_s.at[2 * part, d], recv_sem=tile_r.at[2 * part, d],
+                device_id=(slab, peer), device_id_type=MESH))
+        for c in started:
+            c.start()
+        return started
+
+    def sum_slab_start(part, before):
+        pay, rb1, s1, rb2 = bufs[part][:4]
+        for c in before:
+            c.wait_recv()
+        total = pay[own(part)]
+        for d in range(1, n_tile):
+            total = total + rb1[d]
+        s1[...] = total
+        rb2[slab] = total
+        started = []
+        for d in range(1, n_slab):
+            started.append(pltpu.make_async_remote_copy(
+                src_ref=s1, dst_ref=rb2.at[slab],
+                send_sem=slab_s.at[part, d], recv_sem=slab_r.at[part, d],
+                device_id=(lax.rem(slab + d, n_slab), tile), device_id_type=MESH))
+        for c in started:
+            c.start()
+        return started
+
+    def spread_start(part, before):
+        rb2, f1, fb = bufs[part][3:]
+        for c in before:
+            c.wait_recv()
+        total = rb2[0]
+        for z in range(1, n_slab):
+            total = total + rb2[z]
+        count = jnp.sum((table_v[...] >= 0).astype(F32), axis=0, keepdims=True)
+        count = jnp.sum(jnp.sum(count, axis=2, keepdims=True), axis=1, keepdims=True)[0]
+        total = total / jnp.sqrt(count * 512.0)
+        f1[...] = total
+        fb[own(part)] = total
+        started = []
+        for d in range(1, n_tile):
+            started.append(pltpu.make_async_remote_copy(
+                src_ref=f1, dst_ref=fb.at[own(part)],
+                send_sem=tile_s.at[2 * part + 1, d], recv_sem=tile_r.at[2 * part + 1, d],
+                device_id=(slab, lax.rem(tile + d, n_tile)), device_id_type=MESH))
+        for c in started:
+            c.start()
+        return started
+
+    def finish(part, before):
+        fb = bufs[part][5]
+        for c in before:
+            c.wait_recv()
+        for p, (ke, ko) in enumerate(pairs_of(part)):
+            both = fb[p * 64:(p + 1) * 64]
+            gw_ref[:, ke * 64:ke * 64 + 64] = both[:, 0:64]
+            if ko is not None:
+                gw_ref[:, ko * 64:ko * 64 + 64] = both[:, 64:128]
+
+    all_terms(0)
+    a1 = sum_tile_start(0)
+    all_terms(1)
+    b1 = sum_tile_start(1)
+    second_of(0, c_even, 0)
+    a2 = sum_slab_start(0, a1)
+    second_of(1, c_odd, 0)
+    second_of(2, c_even, 1)
+    b2 = sum_slab_start(1, b1)
+    second_of(3, c_odd, 1)
+    a3 = spread_start(0, a2)
     second_of(4, c_even, 2)
-    for c in step2:
-        c.wait_recv()
-    mine = pl.ds(pl.multiple_of(slab * ch2, 8), ch2)
-    total = s1[mine]
-    for d in range(1, n_slab):
-        total = total + rb2[d]
-    count = jnp.sum((table_v[...] >= 0).astype(F32), axis=0, keepdims=True)
-    count = jnp.sum(jnp.sum(count, axis=2, keepdims=True), axis=1, keepdims=True)[0]
-    f1[mine] = total / jnp.sqrt(count * 512.0)
-
-    step3 = []
-    for d in range(1, n_slab):
-        step3.append(pltpu.make_async_remote_copy(
-            src_ref=f1.at[mine], dst_ref=f1.at[mine],
-            send_sem=c_s.at[d], recv_sem=c_r.at[d],
-            device_id=(lax.rem(slab + d, n_slab), tile), device_id_type=MESH))
-    for c in step3:
-        c.start()
     second_of(5, c_odd, 2)
-    for c in step3:
-        c.wait_recv()
-
-    place = pl.ds(pl.multiple_of(tile * ch1, 8), ch1)
-    step4 = []
-    for d in range(1, n_tile):
-        step4.append(pltpu.make_async_remote_copy(
-            src_ref=f1, dst_ref=fb.at[place],
-            send_sem=e_s.at[d], recv_sem=e_r.at[d],
-            device_id=(slab, lax.rem(tile + d, n_tile)), device_id_type=MESH))
-    for c in step4:
-        c.start()
-    fb[place] = f1[...]
-    lax.fori_loop(3, 4, second, 0)
-    for c in step4:
-        c.wait_recv()
-    for p in range(PAIRS - 1):
-        gw_ref[:, p * 128:(p + 1) * 128] = fb[p * 64:(p + 1) * 64]
-    gw_ref[:, (PAIRS - 1) * 128:] = fb[(PAIRS - 1) * 64:PAIRS * 64, 0:64]
-
-    for c in step1 + step2 + step3 + step4:
+    b3 = spread_start(1, b2)
+    second_of(6, c_even, 3)
+    second_of(7, c_odd, 3)
+    finish(0, a3)
+    finish(1, b3)
+
+    for c in a1 + b1 + a2 + b2 + a3 + b3:
         c.wait_send()
     for m in dirs:
         @pl.when(has(*m))
@@ -313,22 +348,30 @@
 
 def shards(n_slab, n_tile, features, cotangent, weight, block_table):
     table = jnp.transpose(block_table, (0, 2, 1))
-    unit = 8 * n_slab * n_tile
-    rows = -(-PAIRS * 64 // unit) * unit
-    ch1 = rows // n_tile
-    ch2 = ch1 // n_slab
     vmem = pl.BlockSpec(memory_space=pltpu.VMEM)
     smem = pl.BlockSpec(memory_space=pltpu.SMEM)
     dma = pltpu.SemaphoreType.DMA
+    sums = []
+    for part in range(2):
+        rows = rows_of(part, n_tile)
+        ch = rows // n_tile
+        sums += [
+            pltpu.VMEM((rows, 128), F32),
+            pltpu.VMEM((n_tile, ch, 128), F32),
+            pltpu.VMEM((ch, 128), F32),
+            pltpu.VMEM((n_slab, ch, 128), F32),
+            pltpu.VMEM((ch, 128), F32),
+            pltpu.VMEM((rows, 128), F32),
+        ]
     flops = 2 * SLOTS * 640 * 1152 * (384 + 192)
     return pl.pallas_call(
-        functools.partial(kernel, n_slab, n_tile, rows),
+        functools.partial(kernel, n_slab, n_tile),
         out_shape=(
             jax.ShapeDtypeStruct((SLOTS, CH, 512), BF16),
             jax.ShapeDtypeStruct((SLOTS, CH, 512), BF16),
             jax.ShapeDtypeStruct((CH, 27 * CH), F32),
         ),
-        in_specs=[smem] + [pl.BlockSpec(memory_space=pltpu.HBM)] * 4,
+        in_specs=[smem] + [pl.BlockSpec(memory_space=pl.ANY)] * 4,
         out_specs=(vmem, vmem, vmem),
         scratch_shapes=[
             pltpu.VMEM((SLOTS, CH, 512), BF16),
@@ -350,20 +393,13 @@
             pltpu.VMEM((2, CAPL + 1, 64, 128), BF16),
             pltpu.VMEM((2, 2, CAPL, 8, 128), F32),
             pltpu.VMEM((2, 2, CAPL + 1, 8, 128), F32),
-            pltpu.VMEM((rows, 128), F32),
-            pltpu.VMEM((n_tile, ch1, 128), F32),
-            pltpu.VMEM((ch1, 128), F32),
-            pltpu.VMEM((n_slab, ch2, 128), F32),
-            pltpu.VMEM((ch1, 128), F32),
-            pltpu.VMEM((rows, 128), F32),
+            *sums,
             dma((8,)), dma((8,)),
-            dma((n_tile,)), dma((n_tile,)),
-            dma((n_slab,)), dma((n_slab,)),
-            dma((n_slab,)), dma((n_slab,)),
-            dma((n_tile,)), dma((n_tile,)),
+            dma((4, n_tile)), dma((4, n_tile)),
+            dma((2, n_slab)), dma((2, n_slab)),
         ],
         compiler_params=pltpu.CompilerParams(
-            collective_id=0, has_side_effects=True, vmem_limit_bytes=48 * 1024 * 1024
+            collective_id=0, has_side_effects=True, vmem_limit_bytes=60 * 1024 * 1024
         ),
         cost_estimate=pl.CostEstimate(flops=flops, bytes_accessed=3 << 20, transcendentals=0),
     )(table, features, cotangent, weight, table)

time: 46.8 us -> 38.7 us (0.83)
  Pallas kernels: 39.7 us -> 33.9 us
  local copies, waits for them, and re-layouts: 6.09 us -> 3.9 us
    pallas_call x1, Pallas kernels: 39.7 us -> 33.9 us  [shards(): pl.pallas_call(functools.partial(kernel, n_slab, n_tile), out_shape=(jax....]
    unnamed x11 -> x7, local copies, waits for them, and re-layouts: 6.09 us -> 3.9 us
where the time goes in v2:
time: 38.7 us; the launch traced here: 38.4 us
  Pallas kernels  33.9 us (88%)
  local copies, waits for them, and re-layouts  3.9 us (10%)
  between operations  0.65 us (2%)
    pallas_call x1, Pallas kernels, shards(): pl.pallas_call(functools.partial(kernel, n_slab, n_tile), out_shape=(jax....  33.9 us
    unnamed x7, local copies, waits for them, and re-layouts  3.9 us

profile of v2, /device:TPU:0, one launch (start us, length us, event | category | flops | bytes accessed | tf_op | source)
XLA Modules:
  0.0 38.4 jit_solution(13853330858005782892)
XLA Ops:
  0.6 33.9 %shard_map.67 = (bf16[8,64,512]{2,1,0:T(8,128)(2,1)}, bf16[8,64,512]{2,1,0:T(8,128)(2,1)}, f32[64,1728]{1,0:T(8,128)}) custom-call(s32[4,8,16]{2,1,0:T(8,128)} %bitcast.1, bf16[8,64,512]{2,1,0:T(8,128)(2,1)} %x_any.1, bf16[8,64,512]{2,1,0:T(8,128)(2,1)} %g_any.1, bf16[64,1728]{1,0:T(8,128)(2,1)} %w_any.1, s32[4,8,16]{2,1,0:T(8,128)} %bitcast.2), custom_call_target="tpu_custom_call" | custom-call | flops 6794772480 | bytes 3145728 | tf_op jit(solution)/shard_map/pallas_call | solution.py:367
  34.5 0.0 copy-start
  34.5 1.9 %copy.10 = bf16[8,64,512]{2,1,0:T(8,128)(2,1)} copy(bf16[8,64,512]{2,1,0:T(8,128)(2,1)} %get-tuple-element.6) | data formatting | bytes 1048576
  36.4 0.0 copy-done
  36.4 0.0 copy-start.1
  36.4 0.8 %copy.11 = bf16[8,64,512]{2,1,0:T(8,128)(2,1)} copy(bf16[8,64,512]{2,1,0:T(8,128)(2,1)S(1)} %copy-done) | data formatting | bytes 1048576
  37.2 0.4 %copy-done.1 = f32[64,1728]{1,0:T(8,128)S(1)} copy-done((f32[64,1728]{1,0:T(8,128)S(1)}, f32[64,1728]{1,0:T(8,128)}, u32[]{:S(2)}) %copy-start.1) | copy-done | bytes 442392
  37.6 0.8 %copy.12 = f32[64,1728]{1,0:T(8,128)} copy(f32[64,1728]{1,0:T(8,128)S(1)} %copy-done.1) | data formatting | bytes 884736
Async XLA Ops:
  34.5 1.9 %copy-start = (bf16[8,64,512]{2,1,0:T(8,128)(2,1)S(1)}, bf16[8,64,512]{2,1,0:T(8,128)(2,1)}, u32[]{:S(2)}) copy-start(bf16[8,64,512]{2,1,0:T(8,128)(2,1)} %get-tuple-element.7) | copy-start | bytes 1572868
  36.4 1.2 %copy-start.1 = (f32[64,1728]{1,0:T(8,128)S(1)}, f32[64,1728]{1,0:T(8,128)}, u32[]{:S(2)}) copy-start(f32[64,1728]{1,0:T(8,128)} %get-tuple-element.8) | copy-start | bytes 1327108

commit v3 on v2

--- a/solution.py
+++ b/solution.py
@@ -14,30 +14,24 @@
 CH = 64
 SLOTS = LZ * YR * CAPL
 PAIRS = 14
-SHIFTS = ((0, 1, 2, 3, 4), (5, 6, 7, 8))
-
-
-def pairs_of(part):
-    ks = sorted(9 * dz + j for dz in range(3) for j in SHIFTS[part])
-    evens = [k for k in ks if k % 2 == 0]
-    odds = [k for k in ks if k % 2]
-    return [(k, odds[i] if i < len(odds) else None) for i, k in enumerate(evens)]
-
-
-def rows_of(part, n_tile):
-    unit = 8 * n_tile
-    return -(-len(pairs_of(part)) * 64 // unit) * unit
-
 MESH = pl.DeviceIdType.MESH
 F32 = jnp.float32
 BF16 = jnp.bfloat16
+PAIRED = (((1, 0), (4, 3), (7, 6)), ((2, 5), (8, None)))
+ALL_PAIRS = PAIRED[0] + PAIRED[1]
+HALF = len(ALL_PAIRS) * 128
+
+
+def rows_of(part, n_tile):
+    unit = 8 * n_tile
+    return -(-len(PAIRED[part]) * 192 // unit) * unit
 
 
 def kernel(n_slab, n_tile,
            table, x_any, g_any, w_any, table_any,
            conv_ref, grad_ref, gw_ref,
-           x_ref, g_ref, w_ref, table_v, in_sem, pos, valid, w_big,
-           t_buf, d_buf, c_even, c_odd, acc, zs, zr, ys, yr, es, er,
+           x_ref, g_ref, w_ref, table_v, in_sem, pos, valid, w_x, w_g,
+           t_buf, d_buf, c_even, c_odd, f_all, h_all, zs, zr, ys, yr, es, er,
            pay_a, rb1_a, s1_a, rb2_a, f1_a, fb_a,
            pay_b, rb1_b, s1_b, rb2_b, f1_b, fb_b,
            hs_sem, hr_sem, tile_s, tile_r, slab_s, slab_r):
@@ -91,32 +85,35 @@
         es[0, y_side, q] = r4[0, yrow]
         es[1, y_side, q] = r4[7, yrow]
 
-    for c in loads[:2]:
-        c.wait()
-    for s in range(SLOTS):
-        to_rows(s, s // CAPL)
-
-    z_near = (slab > 0).astype(jnp.int32) + (slab < n_slab - 1).astype(jnp.int32)
-    t_near = (tile > 0).astype(jnp.int32) + (tile < n_tile - 1).astype(jnp.int32)
-    pl.semaphore_wait(barrier, n_tile - 1 + n_slab - 1 + z_near * t_near)
-
     dirs = [(dz, dt) for dz in (-1, 0, 1) for dt in (-1, 0, 1) if dz or dt]
     copies = {}
     for m, (dz, dt) in enumerate(dirs):
         zi, yi = (dz + 1) // 2, (dt + 1) // 2
         if dt == 0:
-            src, dst = zs.at[zi], zr.at[1 - zi, pl.ds(0, SLOTS)]
+            spans = [pl.ds(h * CAPL, CAPL) for h in range(YR)]
+            refs = [(zs.at[zi, q], zr.at[1 - zi, q]) for q in spans]
         elif dz == 0:
-            src, dst = ys.at[yi], yr.at[1 - yi, pl.ds(0, CAPL)]
+            refs = [(ys.at[yi], yr.at[1 - yi, pl.ds(0, CAPL)])]
         else:
-            src, dst = es.at[zi, yi], er.at[1 - zi, 1 - yi, pl.ds(0, CAPL)]
-        copies[(dz, dt)] = pltpu.make_async_remote_copy(
-            src_ref=src, dst_ref=dst, send_sem=hs_sem.at[m], recv_sem=hr_sem.at[7 - m],
-            device_id=(slab + dz, tile + dt), device_id_type=MESH)
-    for m in dirs:
-        @pl.when(has(*m))
-        def _():
-            copies[m].start()
+            refs = [(es.at[zi, yi], er.at[1 - zi, 1 - yi, pl.ds(0, CAPL)])]
+        copies[(dz, dt)] = [pltpu.make_async_remote_copy(
+            src_ref=src, dst_ref=dst, send_sem=hs_sem.at[m, h], recv_sem=hr_sem.at[7 - m, h],
+            device_id=(slab + dz, tile + dt), device_id_type=MESH) for h, (src, dst) in enumerate(refs)]
+
+    for c in loads[:2]:
+        c.wait()
+    for h in range(YR):
+        for s in range(h * CAPL, (h + 1) * CAPL):
+            to_rows(s, h)
+        if h == 0:
+            z_near = (slab > 0).astype(jnp.int32) + (slab < n_slab - 1).astype(jnp.int32)
+            t_near = (tile > 0).astype(jnp.int32) + (tile < n_tile - 1).astype(jnp.int32)
+            pl.semaphore_wait(barrier, n_tile - 1 + n_slab - 1 + z_near * t_near)
+        for m in dirs:
+            if m[1] in (0, 2 * h - 1):
+                @pl.when(has(*m))
+                def _():
+                    copies[m][h if m[1] == 0 else 0].start()
 
     for s in range(SLOTS):
         at, found = jnp.int32(0), jnp.float32(0)
@@ -129,24 +126,36 @@
 
     for c in loads[2:]:
         c.wait()
-    wide_lane = lax.broadcasted_iota(jnp.int32, (CH, 128), 1)
+    low = lax.broadcasted_iota(jnp.int32, (CH, 128), 1) < 64
     for p in range(PAIRS):
         if p < PAIRS - 1:
             pair = w_ref[:, p * 128:(p + 1) * 128].astype(F32)
         else:
             pair = jnp.concatenate(
                 [w_ref[:, p * 128:27 * CH].astype(F32), jnp.zeros((CH, 64), F32)], axis=1)
-        flipped = jnp.concatenate([pair, jnp.zeros((CH, 128), F32)], axis=0).T
-        for k in (2 * p, 2 * p + 1):
-            if k >= 27:
+        f_all[p * 128:(p + 1) * 128] = jnp.concatenate([pair, jnp.zeros((CH, 128), F32)], axis=0).T
+        h_all[p * 128:p * 128 + 64] = jnp.where(low, pair, 0.0)
+        h_all[p * 128 + 64:(p + 1) * 128] = jnp.where(low, pltpu.roll(pair, 64, 1), 0.0)
+
+    def turned(k):
+        return f_all[k * 64:(k + 1) * 64]
+
+    def straight(k):
+        return h_all[k * 64:(k + 1) * 64]
+
+    for p, pair in enumerate(ALL_PAIRS):
+        for at, j in enumerate(pair):
+            x_rows = pl.ds(p * 128 + 64 * at, 64)
+            g_rows = pl.ds(p * 128 + 64 * (1 - at), 64)
+            if j is None:
+                w_x[x_rows] = jnp.zeros((64, 256), BF16)
+                w_g[g_rows] = jnp.zeros((64, 256), BF16)
                 continue
-            dz, j = divmod(k, 9)
-            w_big[j * 128:j * 128 + 64, dz * 128:(dz + 1) * 128] = (
-                flipped[k % 2 * 64:k % 2 * 64 + 64].astype(BF16))
-            dz, j = divmod(26 - k, 9)
-            half = pair if k % 2 else pltpu.roll(pair, 64, 1)
-            w_big[j * 128 + 64:(j + 1) * 128, dz * 128:(dz + 1) * 128] = (
-                jnp.where(wide_lane >= 64, half, 0.0).astype(BF16))
+            w_x[x_rows, 0:128] = jnp.where(low, turned(j), pltpu.roll(turned(9 + j), 64, 1)).astype(BF16)
+            w_x[x_rows, 128:256] = turned(18 + j).astype(BF16)
+            w_g[g_rows, 0:128] = jnp.where(
+                low, straight(17 - j), pltpu.roll(straight(26 - j), 64, 1)).astype(BF16)
+            w_g[g_rows, 128:256] = pltpu.roll(straight(8 - j), 64, 1).astype(BF16)
 
     t_buf[SLOTS] = jnp.zeros((8, 8, 8, 2 * CH), F32)
     for side in range(2):
@@ -173,7 +182,8 @@
     for m in dirs:
         @pl.when(has(*m))
         def _():
-            copies[(-m[0], -m[1])].wait_recv()
+            for c in copies[(-m[0], -m[1])]:
+                c.wait_recv()
 
     def outer(b, _):
         for zi in range(2):
@@ -190,32 +200,43 @@
 
     lax.fori_loop(0, LX, outer, 0)
 
-    acc[...] = jnp.zeros_like(acc)
+    bufs = ((pay_a, rb1_a, s1_a, rb2_a, f1_a, fb_a), (pay_b, rb1_b, s1_b, rb2_b, f1_b, fb_b))
+    pay_a[...] = jnp.zeros_like(pay_a)
+    pay_b[...] = jnp.zeros_like(pay_b)
 
     def build(s, c_ref, q, part):
         b = pos[s]
         y0 = s // CAPL * 8
         row = lax.broadcasted_iota(jnp.int32, (10, 8, 2 * CH), 1)
+        lower = lax.broadcasted_iota(jnp.int32, (10, 8, 2 * CH), 2) < CH
         for z in range(10):
+            def put(p, x_val, g_val):
+                for at, v in ((p * 128, x_val), (HALF + p * 128, g_val)):
+                    c_ref[q, z * 64:(z + 1) * 64, at:at + 128] = v.reshape(64, 2 * CH).astype(BF16)
+
             mid = d_buf[b + 1, z, pl.ds(y0, 10)]
-            left = d_buf[b, z, pl.ds(y0, 10)]
-            right = d_buf[b + 2, z, pl.ds(y0, 10)]
-            shifted = (
-                pltpu.roll(jnp.where(row == 7, left, mid), 1, 1),
-                mid,
-                pltpu.roll(jnp.where(row == 0, right, mid), 7, 1),
-            )
-            for j in SHIFTS[part]:
-                dy, dx = divmod(j, 3)
-                c_ref[q, z * 64:(z + 1) * 64, j * 128:(j + 1) * 128] = (
-                    shifted[dx][dy:dy + 8].reshape(64, 2 * CH).astype(BF16))
+            if part == 0:
+                left = d_buf[b, z, pl.ds(y0, 10)]
+                side = pltpu.roll(pltpu.roll(jnp.where(row == 7, left, mid), 1, 1), CH, 2)
+                x_val = jnp.where(lower, mid, side)
+                g_val = jnp.where(lower, side, mid)
+                for dy in range(3):
+                    put(dy, x_val[dy:dy + 8], g_val[dy:dy + 8])
+            else:
+                right = d_buf[b + 2, z, pl.ds(y0, 10)]
+                one = pltpu.roll(jnp.where(row == 0, right, mid), 7, 1)
+                two = pltpu.roll(one, CH, 2)
+                put(3, jnp.where(lower[0:8], one[0:8], two[1:9]), jnp.where(lower[0:8], two[1:9], one[0:8]))
+                put(4, jnp.where(lower[0:8], one[2:10], 0.0), jnp.where(lower[0:8], 0.0, one[2:10]))
 
     def terms(s, c_ref, q, part):
         g = g_ref[s].astype(F32) * valid[s]
         wide = jnp.concatenate([g, jnp.zeros((CH, 128), F32)], axis=1)
         lhs = jnp.concatenate([wide, pltpu.roll(wide, 64, 1), pltpu.roll(wide, 128, 1)], axis=0).astype(BF16)
-        lo, hi = SHIFTS[part][0] * 128, SHIFTS[part][-1] * 128 + 128
-        acc[:, lo:hi] += jnp.dot(lhs, c_ref[q, :, lo:hi], preferred_element_type=F32)
+        first, many = len(PAIRED[0]) * part, len(PAIRED[part])
+        r = jnp.dot(lhs, c_ref[q, :, first * 128:(first + many) * 128], preferred_element_type=F32)
+        for p in range(many):
+            bufs[part][0][p * 192:(p + 1) * 192] += r[:, p * 128:(p + 1) * 128]
 
     def all_terms(part):
         build(0, c_even, 0, part)
@@ -230,19 +251,16 @@
         lax.fori_loop(0, SLOTS // 2, step, 0)
 
     def second_of(s, c_ref, q):
-        r = jnp.dot(c_ref[q], w_big[...], preferred_element_type=F32)
-        o = (r[0:512, 0:128] + r[64:576, 128:256] + r[128:640, 256:384]) * valid[s]
+        rx = jnp.dot(c_ref[q, :, 0:HALF], w_x[...], preferred_element_type=F32)
+        rg = jnp.dot(c_ref[q, :, HALF:2 * HALF], w_g[...], preferred_element_type=F32)
+        lower = lax.broadcasted_iota(jnp.int32, (512, 128), 1) < CH
+        crossed = jnp.where(lower, rg[64:576, 0:128], rx[64:576, 0:128])
+        o = jnp.where(lower, rx[0:512, 0:128], rg[0:512, 0:128]) + pltpu.roll(crossed, CH, 1)
+        o = (o + (rx[128:640, 128:256] + rg[128:640, 128:256])) * valid[s]
         ot = o.T
         conv_ref[s] = ot[0:CH].astype(BF16)
         grad_ref[s] = ot[CH:2 * CH].astype(BF16)
 
-    lane = lax.broadcasted_iota(jnp.int32, (CH, 128), 1)
-    bufs = ((pay_a, rb1_a, s1_a, rb2_a, f1_a, fb_a), (pay_b, rb1_b, s1_b, rb2_b, f1_b, fb_b))
-
-    def term(k):
-        dz, j = divmod(k, 9)
-        return acc[dz * 64:(dz + 1) * 64, j * 128:(j + 1) * 128]
-
     def chunk(part):
         return rows_of(part, n_tile) // n_tile
 
@@ -251,12 +269,6 @@
 
     def sum_tile_start(part):
         pay, rb1 = bufs[part][:2]
-        used = len(pairs_of(part)) * 64
-        for p, (ke, ko) in enumerate(pairs_of(part)):
-            odd = jnp.zeros((CH, 128), F32) if ko is None else pltpu.roll(term(ko), 64, 1)
-            pay[p * 64:(p + 1) * 64] = jnp.where(lane < 64, term(ke), odd)
-        if rows_of(part, n_tile) > used:
-            pay[used:] = jnp.zeros((rows_of(part, n_tile) - used, 128), F32)
         started = []
         for d in range(1, n_tile):
             peer = lax.rem(tile + d, n_tile)
@@ -313,11 +325,13 @@
         fb = bufs[part][5]
         for c in before:
             c.wait_recv()
-        for p, (ke, ko) in enumerate(pairs_of(part)):
-            both = fb[p * 64:(p + 1) * 64]
-            gw_ref[:, ke * 64:ke * 64 + 64] = both[:, 0:64]
-            if ko is not None:
-                gw_ref[:, ko * 64:ko * 64 + 64] = both[:, 64:128]
+        for p, pair in enumerate(PAIRED[part]):
+            for dz in range(3):
+                both = fb[p * 192 + dz * 64:p * 192 + dz * 64 + 64]
+                for at, j in enumerate(pair):
+                    if j is not None:
+                        k = 9 * dz + j
+                        gw_ref[:, k * 64:k * 64 + 64] = both[:, at * 64:at * 64 + 64]
 
     all_terms(0)
     a1 = sum_tile_start(0)
@@ -343,7 +357,8 @@
     for m in dirs:
         @pl.when(has(*m))
         def _():
-            copies[m].wait_send()
+            for c in copies[m]:
+                c.wait_send()
 
 
 def shards(n_slab, n_tile, features, cotangent, weight, block_table):
@@ -363,7 +378,7 @@
             pltpu.VMEM((ch, 128), F32),
             pltpu.VMEM((rows, 128), F32),
         ]
-    flops = 2 * SLOTS * 640 * 1152 * (384 + 192)
+    flops = 2 * SLOTS * 640 * 640 * (512 + 192)
     return pl.pallas_call(
         functools.partial(kernel, n_slab, n_tile),
         out_shape=(
@@ -381,12 +396,14 @@
             dma((4,)),
             pltpu.SMEM((SLOTS,), jnp.int32),
             pltpu.SMEM((SLOTS,), F32),
-            pltpu.VMEM((1152, 384), BF16),
+            pltpu.VMEM((HALF, 256), BF16),
+            pltpu.VMEM((HALF, 256), BF16),
             pltpu.VMEM((SLOTS + 1, 8, 8, 8, 128), F32),
             pltpu.VMEM((LX + 2, 10, 18, 8, 128), F32),
-            pltpu.VMEM((SLOTS // 2 + 1, 640, 1152), BF16),
-            pltpu.VMEM((SLOTS // 2, 640, 1152), BF16),
-            pltpu.VMEM((192, 1152), F32),
+            pltpu.VMEM((SLOTS // 2 + 1, 640, 2 * HALF), BF16),
+            pltpu.VMEM((SLOTS // 2, 640, 2 * HALF), BF16),
+            pltpu.VMEM((PAIRS * 128, 128), F32),
+            pltpu.VMEM((PAIRS * 128, 128), F32),
             pltpu.VMEM((2, SLOTS, 64, 128), BF16),
             pltpu.VMEM((2, SLOTS + 1, 64, 128), BF16),
             pltpu.VMEM((2, CAPL, 64, 128), BF16),
@@ -394,7 +411,7 @@
             pltpu.VMEM((2, 2, CAPL, 8, 128), F32),
             pltpu.VMEM((2, 2, CAPL + 1, 8, 128), F32),
             *sums,
-            dma((8,)), dma((8,)),
+            dma((8, 2)), dma((8, 2)),
             dma((4, n_tile)), dma((4, n_tile)),
             dma((2, n_slab)), dma((2, n_slab)),
         ],

time: 38.7 us -> 40.2 us (1.039)
  Pallas kernels: 33.9 us -> 35.3 us
    pallas_call x1, Pallas kernels: 33.9 us -> 35.3 us  [shards(): pl.pallas_call(functools.partial(kernel, n_slab, n_tile), out_shape=(jax....]
where the time goes in v3:
time: 40.2 us; the launch traced here: 39.9 us
  Pallas kernels  35.3 us (88%)
  local copies, waits for them, and re-layouts  3.9 us (10%)
  between operations  0.65 us (2%)
    pallas_call x1, Pallas kernels, shards(): pl.pallas_call(functools.partial(kernel, n_slab, n_tile), out_shape=(jax....  35.3 us
    unnamed x7, local copies, waits for them, and re-layouts  3.9 us

profile of v3, /device:TPU:0, one launch (start us, length us, event | category | flops | bytes accessed | tf_op | source)
XLA Modules:
  0.0 39.9 jit_solution(6697213597309855969)
XLA Ops:
  0.6 35.3 %shard_map.67 = (bf16[8,64,512]{2,1,0:T(8,128)(2,1)}, bf16[8,64,512]{2,1,0:T(8,128)(2,1)}, f32[64,1728]{1,0:T(8,128)}) custom-call(s32[4,8,16]{2,1,0:T(8,128)} %bitcast.1, bf16[8,64,512]{2,1,0:T(8,128)(2,1)} %x_any.1, bf16[8,64,512]{2,1,0:T(8,128)(2,1)} %g_any.1, bf16[64,1728]{1,0:T(8,128)(2,1)} %w_any.1, s32[4,8,16]{2,1,0:T(8,128)} %bitcast.2), custom_call_target="tpu_custom_call" | custom-call | flops 4613734400 | bytes 3145728 | tf_op jit(solution)/shard_map/pallas_call | solution.py:382
  36.0 0.0 copy-start
  36.0 1.9 %copy.10 = bf16[8,64,512]{2,1,0:T(8,128)(2,1)} copy(bf16[8,64,512]{2,1,0:T(8,128)(2,1)} %get-tuple-element.6) | data formatting | bytes 1048576
  37.9 0.0 copy-done
  37.9 0.0 copy-start.1
  37.9 0.8 %copy.11 = bf16[8,64,512]{2,1,0:T(8,128)(2,1)} copy(bf16[8,64,512]{2,1,0:T(8,128)(2,1)S(1)} %copy-done) | data formatting | bytes 1048576
  38.7 0.4 %copy-done.1 = f32[64,1728]{1,0:T(8,128)S(1)} copy-done((f32[64,1728]{1,0:T(8,128)S(1)}, f32[64,1728]{1,0:T(8,128)}, u32[]{:S(2)}) %copy-start.1) | copy-done | bytes 442392
  39.1 0.8 %copy.12 = f32[64,1728]{1,0:T(8,128)} copy(f32[64,1728]{1,0:T(8,128)S(1)} %copy-done.1) | data formatting | bytes 884736
Async XLA Ops:
  36.0 1.9 %copy-start = (bf16[8,64,512]{2,1,0:T(8,128)(2,1)S(1)}, bf16[8,64,512]{2,1,0:T(8,128)(2,1)}, u32[]{:S(2)}) copy-start(bf16[8,64,512]{2,1,0:T(8,128)(2,1)} %get-tuple-element.7) | copy-start | bytes 1572868
  37.9 1.2 %copy-start.1 = (f32[64,1728]{1,0:T(8,128)S(1)}, f32[64,1728]{1,0:T(8,128)}, u32[]{:S(2)}) copy-start(f32[64,1728]{1,0:T(8,128)} %get-tuple-element.8) | copy-start | bytes 1327108

commit v4 on v2

--- a/solution.py
+++ b/solution.py
@@ -38,9 +38,9 @@
            conv_ref, grad_ref, gw_ref,
            x_ref, g_ref, w_ref, table_v, in_sem, pos, valid, w_big,
            t_buf, d_buf, c_even, c_odd, acc, zs, zr, ys, yr, es, er,
-           pay_a, rb1_a, s1_a, rb2_a, f1_a, fb_a,
-           pay_b, rb1_b, s1_b, rb2_b, f1_b, fb_b,
-           hs_sem, hr_sem, tile_s, tile_r, slab_s, slab_r):
+           pay_a, rb0_a, hs_a, rb1_a, s1_a, rb2_a, fb_a,
+           pay_b, rb0_b, hs_b, rb1_b, s1_b, rb2_b, fb_b,
+           hs_sem, hr_sem, pair_s, pair_r, tile_s, tile_r, slab_s, slab_r, hand_s, hand_r):
     slab = lax.axis_index("slab")
     tile = lax.axis_index("tile")
     def has(dz, dt):
@@ -217,8 +217,9 @@
         lo, hi = SHIFTS[part][0] * 128, SHIFTS[part][-1] * 128 + 128
         acc[:, lo:hi] += jnp.dot(lhs, c_ref[q, :, lo:hi], preferred_element_type=F32)
 
-    def all_terms(part):
-        build(0, c_even, 0, part)
+    def all_terms(part, start, stop):
+        if start == 0:
+            build(0, c_even, 0, part)
 
         def step(q, _):
             terms(2 * q, c_even, q, part)
@@ -227,7 +228,7 @@
             build(jnp.minimum(2 * q + 2, SLOTS - 1), c_even, q + 1, part)
             return 0
 
-        lax.fori_loop(0, SLOTS // 2, step, 0)
+        lax.fori_loop(start, stop, step, 0)
 
     def second_of(s, c_ref, q):
         r = jnp.dot(c_ref[q], w_big[...], preferred_element_type=F32)
@@ -237,7 +238,11 @@
         grad_ref[s] = ot[CH:2 * CH].astype(BF16)
 
     lane = lax.broadcasted_iota(jnp.int32, (CH, 128), 1)
-    bufs = ((pay_a, rb1_a, s1_a, rb2_a, f1_a, fb_a), (pay_b, rb1_b, s1_b, rb2_b, f1_b, fb_b))
+    bufs = ((pay_a, rb0_a, hs_a, rb1_a, s1_a, rb2_a, fb_a), (pay_b, rb0_b, hs_b, rb1_b, s1_b, rb2_b, fb_b))
+    chips = n_tile // 2
+    core = lax.rem(tile, 2)
+    chip = tile // 2
+    partner = tile + 1 - 2 * core
 
     def term(k):
         dz, j = divmod(k, 9)
@@ -246,34 +251,51 @@
     def chunk(part):
         return rows_of(part, n_tile) // n_tile
 
-    def own(part):
-        return pl.ds(pl.multiple_of(tile * chunk(part), 8), chunk(part))
-
-    def sum_tile_start(part):
-        pay, rb1 = bufs[part][:2]
+    def place(part, which_core, which_chip):
+        at = (which_core * chips + which_chip) * chunk(part)
+        return pl.ds(pl.multiple_of(at, 8), chunk(part))
+
+    def half(part, which_core):
+        size = chips * chunk(part)
+        return pl.ds(pl.multiple_of(which_core * size, 8), size)
+
+    def sum_pair_start(part):
+        pay, rb0 = bufs[part][:2]
         used = len(pairs_of(part)) * 64
         for p, (ke, ko) in enumerate(pairs_of(part)):
             odd = jnp.zeros((CH, 128), F32) if ko is None else pltpu.roll(term(ko), 64, 1)
             pay[p * 64:(p + 1) * 64] = jnp.where(lane < 64, term(ke), odd)
         if rows_of(part, n_tile) > used:
             pay[used:] = jnp.zeros((rows_of(part, n_tile) - used, 128), F32)
+        c = pltpu.make_async_remote_copy(
+            src_ref=pay.at[half(part, 1 - core)], dst_ref=rb0,
+            send_sem=pair_s.at[part], recv_sem=pair_r.at[part],
+            device_id=(slab, partner), device_id_type=MESH)
+        c.start()
+        return [c]
+
+    def sum_tile_start(part, before):
+        pay, rb0, hs, rb1 = bufs[part][:4]
+        for c in before:
+            c.wait_recv()
+        hs[...] = pay[half(part, core)] + rb0[...]
         started = []
-        for d in range(1, n_tile):
-            peer = lax.rem(tile + d, n_tile)
+        for d in range(1, chips):
+            peer = lax.rem(chip + d, chips)
             started.append(pltpu.make_async_remote_copy(
-                src_ref=pay.at[pl.ds(pl.multiple_of(peer * chunk(part), 8), chunk(part))],
-                dst_ref=rb1.at[d], send_sem=tile_s.at[2 * part, d], recv_sem=tile_r.at[2 * part, d],
-                device_id=(slab, peer), device_id_type=MESH))
+                src_ref=hs.at[place(part, 0, peer)], dst_ref=rb1.at[d],
+                send_sem=tile_s.at[2 * part, d], recv_sem=tile_r.at[2 * part, d],
+                device_id=(slab, 2 * peer + core), device_id_type=MESH))
         for c in started:
             c.start()
         return started
 
     def sum_slab_start(part, before):
-        pay, rb1, s1, rb2 = bufs[part][:4]
+        hs, rb1, s1, rb2 = bufs[part][2:6]
         for c in before:
             c.wait_recv()
-        total = pay[own(part)]
-        for d in range(1, n_tile):
+        total = hs[place(part, 0, chip)]
+        for d in range(1, chips):
             total = total + rb1[d]
         s1[...] = total
         rb2[slab] = total
@@ -287,8 +309,18 @@
             c.start()
         return started
 
+    def hand(part, d):
+        fb = bufs[part][6]
+        at = place(part, core, lax.rem(chip + chips - d, chips))
+        c = pltpu.make_async_remote_copy(
+            src_ref=fb.at[at], dst_ref=fb.at[at],
+            send_sem=hand_s.at[part, d], recv_sem=hand_r.at[part, d],
+            device_id=(slab, partner), device_id_type=MESH)
+        c.start()
+        return c
+
     def spread_start(part, before):
-        rb2, f1, fb = bufs[part][3:]
+        rb2, fb = bufs[part][5:]
         for c in before:
             c.wait_recv()
         total = rb2[0]
@@ -296,21 +328,28 @@
             total = total + rb2[z]
         count = jnp.sum((table_v[...] >= 0).astype(F32), axis=0, keepdims=True)
         count = jnp.sum(jnp.sum(count, axis=2, keepdims=True), axis=1, keepdims=True)[0]
-        total = total / jnp.sqrt(count * 512.0)
-        f1[...] = total
-        fb[own(part)] = total
+        mine = place(part, core, chip)
+        fb[mine] = total / jnp.sqrt(count * 512.0)
         started = []
-        for d in range(1, n_tile):
+        for d in range(1, chips):
+            peer = lax.rem(chip + d, chips)
             started.append(pltpu.make_async_remote_copy(
-                src_ref=f1, dst_ref=fb.at[own(part)],
+                src_ref=fb.at[mine], dst_ref=fb.at[mine],
                 send_sem=tile_s.at[2 * part + 1, d], recv_sem=tile_r.at[2 * part + 1, d],
-                device_id=(slab, lax.rem(tile + d, n_tile)), device_id_type=MESH))
+                device_id=(slab, 2 * peer + core), device_id_type=MESH))
         for c in started:
             c.start()
+        return started, hand(part, 0)
+
+    def hand_on(part, before):
+        started = []
+        for d, c in enumerate(before, 1):
+            c.wait_recv()
+            started.append(hand(part, d))
         return started
 
     def finish(part, before):
-        fb = bufs[part][5]
+        fb = bufs[part][6]
         for c in before:
             c.wait_recv()
         for p, (ke, ko) in enumerate(pairs_of(part)):
@@ -319,26 +358,31 @@
             if ko is not None:
                 gw_ref[:, ko * 64:ko * 64 + 64] = both[:, 64:128]
 
-    all_terms(0)
-    a1 = sum_tile_start(0)
-    all_terms(1)
-    b1 = sum_tile_start(1)
+    all_terms(0, 0, SLOTS // 2)
+    a0 = sum_pair_start(0)
+    all_terms(1, 0, SLOTS // 4)
+    a1 = sum_tile_start(0, a0)
+    all_terms(1, SLOTS // 4, SLOTS // 2)
+    b0 = sum_pair_start(1)
     second_of(0, c_even, 0)
+    b1 = sum_tile_start(1, b0)
     a2 = sum_slab_start(0, a1)
     second_of(1, c_odd, 0)
     second_of(2, c_even, 1)
     b2 = sum_slab_start(1, b1)
     second_of(3, c_odd, 1)
-    a3 = spread_start(0, a2)
+    a3, a4 = spread_start(0, a2)
     second_of(4, c_even, 2)
+    a5 = hand_on(0, a3)
     second_of(5, c_odd, 2)
-    b3 = spread_start(1, b2)
+    b3, b4 = spread_start(1, b2)
     second_of(6, c_even, 3)
     second_of(7, c_odd, 3)
-    finish(0, a3)
-    finish(1, b3)
-
-    for c in a1 + b1 + a2 + b2 + a3 + b3:
+    b5 = hand_on(1, b3)
+    finish(0, [a4] + a5)
+    finish(1, [b4] + b5)
+
+    for c in a0 + a1 + a2 + a3 + [a4] + a5 + b0 + b1 + b2 + b3 + [b4] + b5:
         c.wait_send()
     for m in dirs:
         @pl.when(has(*m))
@@ -357,10 +401,11 @@
         ch = rows // n_tile
         sums += [
             pltpu.VMEM((rows, 128), F32),
-            pltpu.VMEM((n_tile, ch, 128), F32),
+            pltpu.VMEM((rows // 2, 128), F32),
+            pltpu.VMEM((rows // 2, 128), F32),
+            pltpu.VMEM((n_tile // 2, ch, 128), F32),
             pltpu.VMEM((ch, 128), F32),
             pltpu.VMEM((n_slab, ch, 128), F32),
-            pltpu.VMEM((ch, 128), F32),
             pltpu.VMEM((rows, 128), F32),
         ]
     flops = 2 * SLOTS * 640 * 1152 * (384 + 192)
@@ -395,8 +440,10 @@
             pltpu.VMEM((2, 2, CAPL + 1, 8, 128), F32),
             *sums,
             dma((8,)), dma((8,)),
-            dma((4, n_tile)), dma((4, n_tile)),
+            dma((2,)), dma((2,)),
+            dma((4, n_tile // 2)), dma((4, n_tile // 2)),
             dma((2, n_slab)), dma((2, n_slab)),
+            dma((2, n_tile // 2)), dma((2, n_tile // 2)),
         ],
         compiler_params=pltpu.CompilerParams(
             collective_id=0, has_side_effects=True, vmem_limit_bytes=60 * 1024 * 1024

time: 38.7 us -> 40.9 us (1.057)
  Pallas kernels: 33.9 us -> 36.1 us
    pallas_call x1, Pallas kernels: 33.9 us -> 36.1 us  [shards(): pl.pallas_call(functools.partial(kernel, n_slab, n_tile), out_shape=(jax....]
where the time goes in v4:
time: 40.9 us; the launch traced here: 40.6 us
  Pallas kernels  36.1 us (88%)
  local copies, waits for them, and re-layouts  3.9 us (10%)
  between operations  0.65 us (2%)
    pallas_call x1, Pallas kernels, shards(): pl.pallas_call(functools.partial(kernel, n_slab, n_tile), out_shape=(jax....  36.1 us
    unnamed x7, local copies, waits for them, and re-layouts  3.9 us

profile of v4, /device:TPU:0, one launch (start us, length us, event | category | flops | bytes accessed | tf_op | source)
XLA Modules:
  0.0 40.6 jit_solution(11709114344112863094)
XLA Ops:
  0.6 36.1 %shard_map.67 = (bf16[8,64,512]{2,1,0:T(8,128)(2,1)}, bf16[8,64,512]{2,1,0:T(8,128)(2,1)}, f32[64,1728]{1,0:T(8,128)}) custom-call(s32[4,8,16]{2,1,0:T(8,128)} %bitcast.1, bf16[8,64,512]{2,1,0:T(8,128)(2,1)} %x_any.1, bf16[8,64,512]{2,1,0:T(8,128)(2,1)} %g_any.1, bf16[64,1728]{1,0:T(8,128)(2,1)} %w_any.1, s32[4,8,16]{2,1,0:T(8,128)} %bitcast.2), custom_call_target="tpu_custom_call" | custom-call | flops 6794772480 | bytes 3145728 | tf_op jit(solution)/shard_map/pallas_call | solution.py:412
  36.7 0.0 copy-start
  36.7 1.9 %copy.10 = bf16[8,64,512]{2,1,0:T(8,128)(2,1)} copy(bf16[8,64,512]{2,1,0:T(8,128)(2,1)} %get-tuple-element.6) | data formatting | bytes 1048576
  38.6 0.0 copy-done
  38.6 0.0 copy-start.1
  38.6 0.8 %copy.11 = bf16[8,64,512]{2,1,0:T(8,128)(2,1)} copy(bf16[8,64,512]{2,1,0:T(8,128)(2,1)S(1)} %copy-done) | data formatting | bytes 1048576
  39.4 0.4 %copy-done.1 = f32[64,1728]{1,0:T(8,128)S(1)} copy-done((f32[64,1728]{1,0:T(8,128)S(1)}, f32[64,1728]{1,0:T(8,128)}, u32[]{:S(2)}) %copy-start.1) | copy-done | bytes 442392
  39.8 0.8 %copy.12 = f32[64,1728]{1,0:T(8,128)} copy(f32[64,1728]{1,0:T(8,128)S(1)} %copy-done.1) | data formatting | bytes 884736
Async XLA Ops:
  36.7 1.9 %copy-start = (bf16[8,64,512]{2,1,0:T(8,128)(2,1)S(1)}, bf16[8,64,512]{2,1,0:T(8,128)(2,1)}, u32[]{:S(2)}) copy-start(bf16[8,64,512]{2,1,0:T(8,128)(2,1)} %get-tuple-element.7) | copy-start | bytes 1572868
  38.6 1.2 %copy-start.1 = (f32[64,1728]{1,0:T(8,128)S(1)}, f32[64,1728]{1,0:T(8,128)}, u32[]{:S(2)}) copy-start(f32[64,1728]{1,0:T(8,128)} %get-tuple-element.8) | copy-start | bytes 1327108

commit v5 on v2

--- a/solution.py
+++ b/solution.py
@@ -326,16 +326,16 @@
     second_of(0, c_even, 0)
     a2 = sum_slab_start(0, a1)
     second_of(1, c_odd, 0)
+    b2 = sum_slab_start(1, b1)
     second_of(2, c_even, 1)
-    b2 = sum_slab_start(1, b1)
     second_of(3, c_odd, 1)
     a3 = spread_start(0, a2)
+    b3 = spread_start(1, b2)
     second_of(4, c_even, 2)
     second_of(5, c_odd, 2)
-    b3 = spread_start(1, b2)
     second_of(6, c_even, 3)
+    finish(0, a3)
     second_of(7, c_odd, 3)
-    finish(0, a3)
     finish(1, b3)
 
     for c in a1 + b1 + a2 + b2 + a3 + b3:

time: 38.7 us -> 38.7 us (level)
  no operation moved by 1% of the time
where the time goes in v5:
time: 38.7 us; the launch traced here: 38.4 us
  Pallas kernels  33.9 us (88%)
  local copies, waits for them, and re-layouts  3.9 us (10%)
  between operations  0.65 us (2%)
    pallas_call x1, Pallas kernels, shards(): pl.pallas_call(functools.partial(kernel, n_slab, n_tile), out_shape=(jax....  33.9 us
    unnamed x7, local copies, waits for them, and re-layouts  3.9 us

profile of v5, /device:TPU:0, one launch (start us, length us, event | category | flops | bytes accessed | tf_op | source)
XLA Modules:
  0.0 38.4 jit_solution(8726092129348134525)
XLA Ops:
  0.6 33.9 %shard_map.67 = (bf16[8,64,512]{2,1,0:T(8,128)(2,1)}, bf16[8,64,512]{2,1,0:T(8,128)(2,1)}, f32[64,1728]{1,0:T(8,128)}) custom-call(s32[4,8,16]{2,1,0:T(8,128)} %bitcast.1, bf16[8,64,512]{2,1,0:T(8,128)(2,1)} %x_any.1, bf16[8,64,512]{2,1,0:T(8,128)(2,1)} %g_any.1, bf16[64,1728]{1,0:T(8,128)(2,1)} %w_any.1, s32[4,8,16]{2,1,0:T(8,128)} %bitcast.2), custom_call_target="tpu_custom_call" | custom-call | flops 6794772480 | bytes 3145728 | tf_op jit(solution)/shard_map/pallas_call | solution.py:367
  34.5 0.0 copy-start
  34.5 1.9 %copy.10 = bf16[8,64,512]{2,1,0:T(8,128)(2,1)} copy(bf16[8,64,512]{2,1,0:T(8,128)(2,1)} %get-tuple-element.6) | data formatting | bytes 1048576
  36.4 0.0 copy-done
  36.4 0.0 copy-start.1
  36.4 0.8 %copy.11 = bf16[8,64,512]{2,1,0:T(8,128)(2,1)} copy(bf16[8,64,512]{2,1,0:T(8,128)(2,1)S(1)} %copy-done) | data formatting | bytes 1048576
  37.2 0.4 %copy-done.1 = f32[64,1728]{1,0:T(8,128)S(1)} copy-done((f32[64,1728]{1,0:T(8,128)S(1)}, f32[64,1728]{1,0:T(8,128)}, u32[]{:S(2)}) %copy-start.1) | copy-done | bytes 442392
  37.6 0.8 %copy.12 = f32[64,1728]{1,0:T(8,128)} copy(f32[64,1728]{1,0:T(8,128)S(1)} %copy-done.1) | data formatting | bytes 884736
Async XLA Ops:
  34.5 1.9 %copy-start = (bf16[8,64,512]{2,1,0:T(8,128)(2,1)S(1)}, bf16[8,64,512]{2,1,0:T(8,128)(2,1)}, u32[]{:S(2)}) copy-start(bf16[8,64,512]{2,1,0:T(8,128)(2,1)} %get-tuple-element.7) | copy-start | bytes 1572868
  36.4 1.2 %copy-start.1 = (f32[64,1728]{1,0:T(8,128)S(1)}, f32[64,1728]{1,0:T(8,128)}, u32[]{:S(2)}) copy-start(f32[64,1728]{1,0:T(8,128)} %get-tuple-element.8) | copy-start | bytes 1327108

commit v6 on v5

--- a/solution.py
+++ b/solution.py
@@ -268,7 +268,21 @@
             c.start()
         return started
 
-    def sum_slab_start(part, before):
+    def slab_copies(part):
+        s1, rb2 = bufs[part][2:4]
+        return [pltpu.make_async_remote_copy(
+            src_ref=s1, dst_ref=rb2.at[slab],
+            send_sem=slab_s.at[part, d], recv_sem=slab_r.at[part, d],
+            device_id=(lax.rem(slab + d, n_slab), tile), device_id_type=MESH) for d in range(1, n_slab)]
+
+    def spread_copies(part):
+        f1, fb = bufs[part][4:]
+        return [pltpu.make_async_remote_copy(
+            src_ref=f1, dst_ref=fb.at[own(part)],
+            send_sem=tile_s.at[2 * part + 1, d], recv_sem=tile_r.at[2 * part + 1, d],
+            device_id=(slab, lax.rem(tile + d, n_tile)), device_id_type=MESH) for d in range(1, n_tile)]
+
+    def sum_slab(part, before, started):
         pay, rb1, s1, rb2 = bufs[part][:4]
         for c in before:
             c.wait_recv()
@@ -277,17 +291,10 @@
             total = total + rb1[d]
         s1[...] = total
         rb2[slab] = total
-        started = []
-        for d in range(1, n_slab):
-            started.append(pltpu.make_async_remote_copy(
-                src_ref=s1, dst_ref=rb2.at[slab],
-                send_sem=slab_s.at[part, d], recv_sem=slab_r.at[part, d],
-                device_id=(lax.rem(slab + d, n_slab), tile), device_id_type=MESH))
         for c in started:
             c.start()
-        return started
-
-    def spread_start(part, before):
+
+    def spread(part, before, started):
         rb2, f1, fb = bufs[part][3:]
         for c in before:
             c.wait_recv()
@@ -299,15 +306,8 @@
         total = total / jnp.sqrt(count * 512.0)
         f1[...] = total
         fb[own(part)] = total
-        started = []
-        for d in range(1, n_tile):
-            started.append(pltpu.make_async_remote_copy(
-                src_ref=f1, dst_ref=fb.at[own(part)],
-                send_sem=tile_s.at[2 * part + 1, d], recv_sem=tile_r.at[2 * part + 1, d],
-                device_id=(slab, lax.rem(tile + d, n_tile)), device_id_type=MESH))
         for c in started:
             c.start()
-        return started
 
     def finish(part, before):
         fb = bufs[part][5]
@@ -323,19 +323,25 @@
     a1 = sum_tile_start(0)
     all_terms(1)
     b1 = sum_tile_start(1)
-    second_of(0, c_even, 0)
-    a2 = sum_slab_start(0, a1)
-    second_of(1, c_odd, 0)
-    b2 = sum_slab_start(1, b1)
-    second_of(2, c_even, 1)
-    second_of(3, c_odd, 1)
-    a3 = spread_start(0, a2)
-    b3 = spread_start(1, b2)
-    second_of(4, c_even, 2)
-    second_of(5, c_odd, 2)
-    second_of(6, c_even, 3)
+    a2, b2, a3, b3 = slab_copies(0), slab_copies(1), spread_copies(0), spread_copies(1)
+
+    def outputs(q, _):
+        second_of(2 * q, c_even, q)
+        second_of(2 * q + 1, c_odd, q)
+
+        @pl.when(q == 0)
+        def _():
+            sum_slab(0, a1, a2)
+            sum_slab(1, b1, b2)
+
+        @pl.when(q == 1)
+        def _():
+            spread(0, a2, a3)
+            spread(1, b2, b3)
+        return 0
+
+    lax.fori_loop(0, SLOTS // 2, outputs, 0)
     finish(0, a3)
-    second_of(7, c_odd, 3)
     finish(1, b3)
 
     for c in a1 + b1 + a2 + b2 + a3 + b3:

time: 38.7 us -> 38.8 us (level)
  no operation moved by 1% of the time
where the time goes in v6:
time: 38.8 us; the launch traced here: 38.6 us
  Pallas kernels  34 us (88%)
  local copies, waits for them, and re-layouts  3.9 us (10%)
  between operations  0.65 us (2%)
    pallas_call x1, Pallas kernels, shards(): pl.pallas_call(functools.partial(kernel, n_slab, n_tile), out_shape=(jax....  34 us
    unnamed x7, local copies, waits for them, and re-layouts  3.9 us

profile of v6, /device:TPU:0, one launch (start us, length us, event | category | flops | bytes accessed | tf_op | source)
XLA Modules:
  0.0 38.6 jit_solution(6738422410997711162)
XLA Ops:
  0.6 34.0 %shard_map.67 = (bf16[8,64,512]{2,1,0:T(8,128)(2,1)}, bf16[8,64,512]{2,1,0:T(8,128)(2,1)}, f32[64,1728]{1,0:T(8,128)}) custom-call(s32[4,8,16]{2,1,0:T(8,128)} %bitcast.1, bf16[8,64,512]{2,1,0:T(8,128)(2,1)} %x_any.1, bf16[8,64,512]{2,1,0:T(8,128)(2,1)} %g_any.1, bf16[64,1728]{1,0:T(8,128)(2,1)} %w_any.1, s32[4,8,16]{2,1,0:T(8,128)} %bitcast.2), custom_call_target="tpu_custom_call" | custom-call | flops 6794772480 | bytes 3145728 | tf_op jit(solution)/shard_map/pallas_call | solution.py:373
  34.6 0.0 copy-start
  34.7 1.9 %copy.10 = bf16[8,64,512]{2,1,0:T(8,128)(2,1)} copy(bf16[8,64,512]{2,1,0:T(8,128)(2,1)} %get-tuple-element.6) | data formatting | bytes 1048576
  36.6 0.0 copy-done
  36.6 0.0 copy-start.1
  36.6 0.8 %copy.11 = bf16[8,64,512]{2,1,0:T(8,128)(2,1)} copy(bf16[8,64,512]{2,1,0:T(8,128)(2,1)S(1)} %copy-done) | data formatting | bytes 1048576
  37.4 0.4 %copy-done.1 = f32[64,1728]{1,0:T(8,128)S(1)} copy-done((f32[64,1728]{1,0:T(8,128)S(1)}, f32[64,1728]{1,0:T(8,128)}, u32[]{:S(2)}) %copy-start.1) | copy-done | bytes 442392
  37.8 0.8 %copy.12 = f32[64,1728]{1,0:T(8,128)} copy(f32[64,1728]{1,0:T(8,128)S(1)} %copy-done.1) | data formatting | bytes 884736
Async XLA Ops:
  34.6 1.9 %copy-start = (bf16[8,64,512]{2,1,0:T(8,128)(2,1)S(1)}, bf16[8,64,512]{2,1,0:T(8,128)(2,1)}, u32[]{:S(2)}) copy-start(bf16[8,64,512]{2,1,0:T(8,128)(2,1)} %get-tuple-element.7) | copy-start | bytes 1572868
  36.6 1.2 %copy-start.1 = (f32[64,1728]{1,0:T(8,128)S(1)}, f32[64,1728]{1,0:T(8,128)}, u32[]{:S(2)}) copy-start(f32[64,1728]{1,0:T(8,128)} %get-tuple-element.8) | copy-start | bytes 1327108
